TPU v7x, 32 devices: a whole 2x2x4 slice. The times are simulated.
32 devices in a mesh: rep: 2 (over y), fsdp: 4 (over z), dp: 2 (over x), sub: 2 (over core).
Axes of the slice: x: 2, y: 2, z: 4, core: 2. Of those that a mesh axis runs over, the one named last changes fastest.
Arguments:
- features: bfloat16 [1024, 4096], P(('rep', 'dp', 'sub'), 'fsdp'), parts along dimension 0, may hold values from -6 to 6
- values: bfloat16 [64, 64, 4864], P('fsdp'), may hold values from -0.15625 to 0.15625
- col_idx: int32 [64, 76], P('fsdp'), may hold values from 0 to 255, as said below
- cotangent: bfloat16 [1024, 16384], P(('rep', 'dp', 'sub'), 'fsdp'), parts along dimension 0, may hold values from -6 to 6
Outputs:
- projected: bfloat16 [1024, 16384], P(('rep', 'dp', 'sub'), 'fsdp'), parts along dimension 0
- input_grad: bfloat16 [1024, 4096], P(('rep', 'dp', 'sub'), 'fsdp'), parts along dimension 0
- weight_grad: float32 [128, 64, 4864], P(('rep', 'fsdp')), parts along dimension 0
There are 2 independent parts, one for each index of `rep`. A program takes and returns all parts, laid end to end along the dimension named above; an argument that names none is the same for every part. Nothing has to cross between parts.
Inputs may be any that keep to these rules, and one draw needn't show every extreme that they name: `col_idx`: each block row lists exactly 76 distinct block columns in ascending order. At most 48 of one block row's columns fall into one aligned group of 64 block columns; in every draw some group holds exactly 48 columns of every block row.
All inputs are finite; a program needn't handle non-finite values.
Results may differ from a plain program's by a relative error of at most 0.0085.
Values may be sent and summed in bfloat16 or wider, within the bound.
A program may use at most 448 MiB of HBM per device.

v0:
```python
import jax
import jax.numpy as jnp
from jax import lax
from jax.sharding import PartitionSpec as P

D = 4096
BS = 64
NBC = 256
KEEP = 76


def grad_rows(rows_part, cotangent):
    product = lax.dot_general(
        rows_part, cotangent, (((0,), (0,)), ((), ())), preferred_element_type=jnp.float32
    )
    return product.astype(jnp.bfloat16)


def body(features, values, col_idx, cotangent):
    tile_count = lax.axis_size("fsdp")
    group = lax.axis_size("dp") * lax.axis_size("sub")
    rows_dev = values.shape[0]
    tile_cols = NBC // tile_count
    tile_width = tile_cols * BS
    values_view = values.reshape(rows_dev, BS, KEEP, BS)
    selector = (col_idx[:, :, None] == jnp.arange(NBC, dtype=jnp.int32)[None, None, :]).astype(
        jnp.bfloat16
    )
    dense_rows = jnp.einsum(
        "rkn,rakb->ranb", selector, values_view, preferred_element_type=jnp.float32
    ).astype(jnp.bfloat16)
    dense_rows = dense_rows.reshape(rows_dev, BS, tile_count, tile_width)
    dense_flat = dense_rows.reshape(rows_dev * BS, tile_count, tile_width)
    weight_tile = lax.all_to_all(
        dense_flat, "fsdp", split_axis=1, concat_axis=0, tiled=True
    ).reshape(D, tile_width)
    collected_rows = lax.all_gather(features, "fsdp", axis=1, tiled=True)
    projected = jnp.dot(collected_rows, weight_tile, preferred_element_type=jnp.float32).astype(
        jnp.bfloat16
    )
    block_rows = min(512, D)
    stacked = collected_rows.reshape(
        collected_rows.shape[0], D // block_rows, block_rows
    ).transpose(1, 0, 2)
    weight_grad_tile = lax.map(lambda rows_part: grad_rows(rows_part, cotangent), stacked).reshape(
        D, tile_width
    )
    input_sum = lax.psum_scatter(
        lax.dot_general(
            weight_tile, cotangent, (((1,), (1,)), ((), ())), preferred_element_type=jnp.float32
        ).astype(jnp.bfloat16),
        "fsdp",
        scatter_dimension=0,
        tiled=True,
    ).astype(jnp.float32)
    input_grad = input_sum.T.astype(jnp.bfloat16)
    returned = lax.all_to_all(
        weight_grad_tile.reshape(D, 1, tile_width), "fsdp", split_axis=0, concat_axis=1, tiled=True
    )
    grid_rows = returned.reshape(rows_dev, BS, NBC, BS)
    own_blocks = jnp.einsum(
        "ranb,rkn->rakb", grid_rows, selector, preferred_element_type=jnp.float32
    ).astype(jnp.bfloat16)
    partial_grad = own_blocks.reshape(rows_dev, BS, KEEP * BS)
    grad_total = lax.psum(partial_grad, ("dp", "sub")).astype(jnp.float32)
    token_count = features.shape[0] * group
    weight_grad = grad_total / jnp.sqrt(jnp.float32(token_count))
    return (projected, input_grad, weight_grad)


def solution(mesh):
    in_specs = (
        P(("rep", "dp", "sub"), "fsdp"),
        P("fsdp", None, None),
        P("fsdp", None),
        P(("rep", "dp", "sub"), "fsdp"),
    )
    out_specs = (
        P(("rep", "dp", "sub"), "fsdp"),
        P(("rep", "dp", "sub"), "fsdp"),
        P(("rep", "fsdp"), None, None),
    )
    return jax.shard_map(body, mesh=mesh, in_specs=in_specs, out_specs=out_specs, check_vma=False)
```

profile of v0, /device:TPU:0, one launch (start us, length us, event | category | flops | bytes accessed | tf_op | source)
XLA Modules:
  0.0 2457.2 jit_solution(725456717212241364)
XLA Ops:
  7.2 0.0 copy-start.1
  7.2 26.2 %reshape.24 = bf16[16,64,76,64]{3,2,1,0:T(8,128)(2,1)} reshape(bf16[16,64,4864]{2,1,0:T(8,128)(2,1)} %param.7) | data formatting | bytes 19922944 | tf_op jit(solution)/shard_map/reshape | solution.py:25
  33.3 24.8 %copy.39 = bf16[16,64,76,64]{2,3,1,0:T(8,128)(2,1)} copy(bf16[16,64,76,64]{3,2,1,0:T(8,128)(2,1)} %reshape.24) | data formatting | bytes 19922944 | tf_op jit(solution)/shard_map/reshape | solution.py:25
  58.1 0.0 copy-done.1
  58.1 28.8 %fusion.7 = f32[16,256,4096]{1,2,0} fusion(bf16[16,76,4096]{1,2,0:T(8,128)(2,1)} %bitcast.58, s32[16,76]{1,0:T(8,128)S(1)} %copy-done.1), kind=kOutput, calls=%fused_computation.14 | convolution fusion | flops 2550448128 | bytes 77075200
  86.9 32.4 %convert_bitcast_fusion = bf16[16,64,256,64]{2,3,1,0:T(8,128)(2,1)} fusion(f32[16,256,64,64]{1,3,2,0:T(8,128)} %bitcast.4), kind=kLoop, calls=%fused_computation.6 | loop fusion | flops 16777216 | bytes 100663296 | tf_op jit(solution)/shard_map/convert_element_type | solution.py:31
  119.3 112.5 %copy.40 = bf16[16,64,256,64]{1,0,3,2:T(8,128)(2,1)} copy(bf16[16,64,256,64]{2,3,1,0:T(8,128)(2,1)} %convert_bitcast_fusion) | data formatting | bytes 67108864 | tf_op jit(solution)/shard_map/convert_element_type | solution.py:31
  231.9 86.9 %reshape_reshape.6 = bf16[1024,4,4096]{0,2,1:T(8,128)(2,1)} reshape(bf16[16,64,256,64]{1,0,3,2:T(8,128)(2,1)} %copy.40) | data formatting | bytes 67108864 | tf_op jit(solution)/shard_map/reshape;reshape | solution.py:33
  318.8 9.8 all-to-all-start
  328.6 0.2 all-gather.2.cloned.1.call-start
  328.9 0.8 copy.42
  329.7 0.0 all-gather.2.cloned.1.call-update
  329.7 210.5 %all-gather.2.cloned.1.call-done = bf16[128,4096]{0,1:T(8,128)(2,1)} async-done(((bf16[128,1024]{0,1:T(8,128)(2,1)}), bf16[128,4096]{0,1:T(8,128)(2,1)}) %all-gather.2.cloned.1.call-update) | async-done | bytes 1048592 | tf_op jit(solution)/shard_map/all_gather | solution.py:37
  540.2 32.9 %while.10 = (s32[]{:T(128)}, bf16[8,512,4096]{2,1,0:T(8,128)(2,1)}, bf16[8,128,512]{1,2,0:T(8,128)(2,1)}, bf16[128,4096]{1,0:T(8,128)(2,1)S(1)}, s32[]{:T(128)}) while((s32[]{:T(128)}, bf16[8,512,4096]{2,1,0:T(8,128)(2,1)}, bf16[8,128,512]{1,2,0:T(8,128)(2,1)}, bf16[128,4096]{1,0:T(8,128)(2,1)S(1)}, s32[]{:T(128)}) %tuple.41), condition=%wide.region_2.3_spmd, body=%wide.region_1.2_spmd.sunk | while | flops 538968064 | bytes 5375045 | solution.py:45
  540.2 4.2 fusion.22
  544.5 4.1 fusion.22
  548.5 4.1 fusion.22
  552.6 4.1 fusion.22
  556.7 4.2 fusion.22
  560.9 4.1 fusion.22
  565.0 4.1 fusion.22
  569.1 4.1 fusion.22
  573.2 0.5 broadcast.2
  573.7 27.8 %reduce = bf16[4096,4096]{1,0:T(8,128)(2,1)} reduce(bf16[4096,1,4096]{2,0,1:T(8,128)(2,1)} %bitcast.59, bf16[]{:T(256)} %broadcast.2), dimensions={1}, to_apply=%copy.44.reduce_sub_computation | reduce | bytes 67108864 | tf_op jit(solution)/shard_map/reshape;reshape | solution.py:58
  601.5 50.5 %reshape.33 = bf16[4,2,2097152]{2,1,0:T(2,128)(2,1)} reshape(bf16[4096,4096]{1,0:T(8,128)(2,1)} %reduce) | data formatting | bytes 67108864
  652.0 417.6 %all-to-all-done = bf16[1024,4,4096]{0,2,1:T(8,128)(2,1)} async-done(((bf16[1024,4,4096]{0,2,1:T(8,128)(2,1)}), bf16[1024,4,4096]{0,2,1:T(8,128)(2,1)}, u32[]{:S(2)}, u32[]{:S(2)}) %all-to-all-start) | async-done | bytes 33554464 | tf_op jit(solution)/shard_map/all_to_all | solution.py:34
  1069.5 9.8 all-to-all-start.1
  1079.3 0.0 reduce-scatter.2.cloned.1.call-start
  1079.4 40.0 %copy.41 = bf16[4,1024,1,4096]{3,1,0,2:T(8,128)(2,1)} copy(bf16[4,1024,1,4096]{1,3,0,2:T(8,128)(2,1)} %bitcast.7) | data formatting | bytes 67108864 | tf_op jit(solution)/shard_map/all_to_all | solution.py:34
  1119.4 16.2 convolution_convert_fusion.1
  1135.6 0.0 reduce-scatter.2.cloned.1.call-update
  1135.6 0.4 all-reduce.2.cloned.1.call-start
  1136.1 682.2 %all-to-all-done.1 = bf16[4,2,2097152]{2,1,0:T(2,128)(2,1)} async-done(((bf16[4,2,2097152]{2,1,0:T(2,128)(2,1)}), bf16[4,2,2097152]{2,1,0:T(2,128)(2,1)}, u32[]{:S(2)}, u32[]{:S(2)}) %all-to-all-start.1) | async-done | bytes 33554464 | tf_op jit(solution)/shard_map/all_to_all | solution.py:57
  1818.3 74.1 %reshape.34 = bf16[4096,1,4096]{2,1,0:T(2,128)(2,1)} reshape(bf16[4,2,2097152]{2,1,0:T(2,128)(2,1)} %all-to-all-done.1) | data formatting | bytes 67108864
  1892.4 57.0 %copy.51 = bf16[4096,1,4096]{2,0,1:T(8,128)(2,1)} copy(bf16[4096,1,4096]{2,1,0:T(2,128)(2,1)} %reshape.34) | data formatting | bytes 67108864
  1949.5 40.6 %copy.45 = bf16[1024,4,1,4096]{0,3,1,2:T(8,128)(2,1)} copy(bf16[1024,4,1,4096]{3,0,1,2:T(8,128)(2,1)} %bitcast.57) | data formatting | bytes 67108864 | tf_op jit(solution)/shard_map/all_to_all | solution.py:57
  1990.0 84.7 %reshape.27 = bf16[16,64,256,64]{1,0,3,2:T(8,128)(2,1)} reshape(bf16[1024,4,1,4096]{0,3,1,2:T(8,128)(2,1)} %copy.45) | data formatting | bytes 67108864 | tf_op jit(solution)/shard_map/reshape | solution.py:60
  2074.7 93.0 %copy.46 = bf16[16,64,256,64]{2,3,1,0:T(8,128)(2,1)} copy(bf16[16,64,256,64]{1,0,3,2:T(8,128)(2,1)} %reshape.27) | data formatting | bytes 67108864 | tf_op jit(solution)/shard_map/reshape | solution.py:60
  2167.7 23.1 fusion.6
  2190.7 18.2 convert_bitcast_fusion.1
  2208.9 24.9 %copy.47 = bf16[16,64,76,64]{3,2,1,0:T(8,128)(2,1)} copy(bf16[16,64,76,64]{2,3,1,0:T(8,128)(2,1)} %convert_bitcast_fusion.1) | data formatting | bytes 19922944 | tf_op jit(solution)/shard_map/convert_element_type | solution.py:63
  2233.8 26.0 %reshape.28 = bf16[16,64,4864]{2,1,0:T(8,128)(2,1)} reshape(bf16[16,64,76,64]{3,2,1,0:T(8,128)(2,1)} %copy.47) | data formatting | bytes 19922944 | tf_op jit(solution)/shard_map/reshape | solution.py:64
  2259.9 0.0 all-reduce.2.cloned.1.call-update
  2259.9 16.2 fusion.5
  2276.1 1.3 copy.48
  2277.4 1.8 copy.49
  2279.2 158.0 %all-reduce.2.cloned.1.call-done = bf16[16,64,4864]{2,1,0:T(8,128)(2,1)} async-done(((bf16[16,64,4864]{2,1,0:T(8,128)(2,1)}), bf16[16,64,4864]{2,1,0:T(8,128)(2,1)}) %all-reduce.2.cloned.1.call-update) | async-done | bytes 9961488 | tf_op jit(solution)/shard_map/psum | solution.py:65
  2437.2 13.3 convert_multiply_fusion
  (10 shorter events, 0.0 us)
Async XLA Ops:
  7.2 51.0 %copy-start.1 = (s32[16,76]{1,0:T(8,128)S(1)}, s32[16,76]{1,0:T(8,128)}, u32[]{:S(2)}) copy-start(s32[16,76]{1,0:T(8,128)} %param.8) | copy-start | bytes 14596
  318.8 10.1 copy-start.4
  318.8 221.5 %copy-start = (bf16[128,4096]{1,0:T(8,128)(2,1)S(1)}, bf16[128,4096]{1,0:T(8,128)(2,1)}, u32[]{:S(2)}) copy-start(bf16[128,4096]{1,0:T(8,128)(2,1)} %param.9) | copy-start | bytes 3145732
  318.8 750.8 %all-to-all-start = ((bf16[1024,4,4096]{0,2,1:T(8,128)(2,1)}), bf16[1024,4,4096]{0,2,1:T(8,128)(2,1)}, u32[]{:S(2)}, u32[]{:S(2)}) async-start(bf16[1024,4,4096]{0,2,1:T(8,128)(2,1)} %reshape_reshape.6), calls=%async_computation | async-start | bytes 67108864 | tf_op jit(solution)/shard_map/all_to_all | solution.py:34
  328.6 211.6 %all-gather.2.cloned.1.call-start = ((), (), s32[]{:S(2)}) async-start(), calls=%async_computation.3 | async-start | bytes 1310720 | tf_op jit(solution)/shard_map/all_gather | solution.py:37
  1069.5 748.8 %all-to-all-start.1 = ((bf16[4,2,2097152]{2,1,0:T(2,128)(2,1)}), bf16[4,2,2097152]{2,1,0:T(2,128)(2,1)}, u32[]{:S(2)}, u32[]{:S(2)}) async-start(bf16[4,2,2097152]{2,1,0:T(2,128)(2,1)} %reshape.33), calls=%async_computation.2 | async-start | bytes 67108864 | tf_op jit(solution)/shard_map/all_to_all | solution.py:57
  1079.3 1198.0 %reduce-scatter.2.cloned.1.call-start = ((), (), s32[]{:S(2)}) async-start(), calls=%async_computation.4 | async-start | bytes 1310720 | tf_op jit(solution)/shard_map/reduce_scatter | solution.py:48
  1135.6 1301.6 %all-reduce.2.cloned.1.call-start = ((), (), s32[]{:S(2)}) async-start(), calls=%async_computation.5 | async-start | bytes 19922944 | tf_op jit(solution)/shard_map/psum | solution.py:65
  2074.7 93.0 %copy-start.2 = (s32[16,76]{1,0:T(8,128)S(1)}, s32[16,76]{1,0:T(8,128)}, u32[]{:S(2)}) copy-start(s32[16,76]{1,0:T(8,128)} %param.8) | copy-start | bytes 14596
  2208.9 51.0 %copy-start.3 = (bf16[8,128,512]{1,2,0:T(8,128)(2,1)S(1)}, bf16[8,128,512]{1,2,0:T(8,128)(2,1)}, u32[]{:S(2)}) copy-start(bf16[8,128,512]{1,2,0:T(8,128)(2,1)} %get-tuple-element.121) | copy-start | bytes 3145732
Sparse Core Ops, SparseCore 0:
  331.6 208.5 all-gather.1
  1135.7 153.5 reduce-scatter.1
  2260.0 177.1 all-reduce.1
where the time goes:
time: 2470 us; the launch traced here: 2460 us
  waiting for transfers between devices  1470 us (60%)
  local copies, waits for them, and re-layouts  746 us (30%)
  matrix products  117 us (5%)
  other arithmetic  91.6 us (4%)
    all_to_all x1, waiting for transfers between devices, body(): lax.all_to_all(weight_grad_tile.reshape(D, 1, tile_width), 'fsdp', split_...  682 us
    all_to_all x1, waiting for transfers between devices, body(): lax.all_to_all(dense_flat, 'fsdp', split_axis=1, concat_axis=0, tiled=True)  418 us
    all_gather x1, waiting for transfers between devices, body(): collected_rows = lax.all_gather(features, 'fsdp', axis=1, tiled=True)  211 us
    unnamed x16, local copies, waits for them, and re-layouts  186 us
    reshape x2, local copies, waits for them, and re-layouts, body(): grid_rows = returned.reshape(rows_dev, BS, NBC, BS)  178 us
    psum x1, waiting for transfers between devices, body(): grad_total = lax.psum(partial_grad, ('dp', 'sub')).astype(jnp.float32)  158 us
    convert_element_type x1, local copies, waits for them, and re-layouts, body(): dense_rows = jnp.einsum('rkn,rakb->ranb', selector, values_view, preferre...  113 us
    another operation x1, local copies, waits for them, and re-layouts, body(): dense_flat = dense_rows.reshape(rows_dev * BS, tile_count, tile_width)  86.9 us
  transfers between devices with their start and end apart: 5, of which 4 were waited for; matrix products, arithmetic and copies ran while one was open for 26% of the time, Pallas kernels for 0%

commit v1 on v0

v1 whole, which is shorter than its diff:
```python
import functools

import jax
import jax.numpy as jnp
from jax import lax
from jax.experimental import pallas as pl
from jax.experimental.pallas import tpu as pltpu
from jax.sharding import PartitionSpec as P

BS = 64
NBC = 256
FF = BS * NBC
VMEM = 60 * 1024 * 1024


def expand_kernel(idx, vt_ref, w_ref):
    pair = pl.program_id(0)
    keep = vt_ref.shape[0] // BS
    chunk = 512

    @pl.loop(0, FF // chunk)
    def _(i):
        w_ref[pl.ds(pl.multiple_of(i * chunk, chunk), chunk), :] = jnp.zeros(
            (chunk, 2 * BS), w_ref.dtype
        )

    lane = lax.broadcasted_iota(jnp.int32, (BS, 2 * BS), 1)
    for half in range(2):
        mask = (lane >= BS) if half else (lane < BS)

        @pl.loop(0, keep, unroll=4)
        def _(k):
            place = pl.ds(pl.multiple_of(idx[2 * pair + half, k] * BS, BS), BS)
            block = vt_ref[pl.ds(pl.multiple_of(k * BS, BS), BS), :]
            w_ref[place, :] = jnp.where(mask, block, w_ref[place, :])


def expand(col_idx, values_t):
    depth, rows = values_t.shape
    return pl.pallas_call(
        expand_kernel,
        out_shape=jax.ShapeDtypeStruct((FF, rows), values_t.dtype),
        grid_spec=pltpu.PrefetchScalarGridSpec(
            num_scalar_prefetch=1,
            grid=(rows // (2 * BS),),
            in_specs=[pl.BlockSpec((depth, 2 * BS), lambda i, idx: (0, i))],
            out_specs=pl.BlockSpec((FF, 2 * BS), lambda i, idx: (0, i)),
        ),
        compiler_params=pltpu.CompilerParams(vmem_limit_bytes=VMEM),
        cost_estimate=pl.CostEstimate(
            flops=0, bytes_accessed=2 * rows * (FF + depth), transcendentals=0
        ),
    )(col_idx, values_t)


def project_kernel(x_ref, w_ref, o_ref):
    o_ref[0] = lax.dot_general(
        x_ref[...], w_ref[...], (((1,), (1,)), ((), ())), preferred_element_type=jnp.float32
    ).astype(o_ref.dtype)


def project(features, weight_t, tiles):
    tokens, rows = features.shape
    width = FF // tiles
    cols = min(2048, width)
    per = width // cols
    return pl.pallas_call(
        project_kernel,
        out_shape=jax.ShapeDtypeStruct((tiles, tokens, width), jnp.bfloat16),
        grid=(tiles, per),
        in_specs=[
            pl.BlockSpec((tokens, rows), lambda f, j: (0, 0)),
            pl.BlockSpec((cols, rows), lambda f, j: (f * per + j, 0)),
        ],
        out_specs=pl.BlockSpec((1, tokens, cols), lambda f, j: (f, 0, j)),
        compiler_params=pltpu.CompilerParams(vmem_limit_bytes=VMEM),
        cost_estimate=pl.CostEstimate(
            flops=2 * tokens * rows * FF, bytes_accessed=2 * FF * (rows + tokens), transcendentals=0
        ),
    )(features, weight_t)


def back_kernel(g_ref, w_ref, o_ref, total):
    f, j = pl.program_id(0), pl.program_id(1)
    first = jnp.logical_and(f == 0, j == 0)
    last = jnp.logical_and(f == pl.num_programs(0) - 1, j == pl.num_programs(1) - 1)

    @pl.when(first)
    def _():
        total[...] = jnp.zeros_like(total)

    total[...] += jnp.dot(g_ref[0], w_ref[...], preferred_element_type=jnp.float32)

    @pl.when(last)
    def _():
        o_ref[...] = total[...].astype(o_ref.dtype)


def back(cotangent, weight_t):
    tiles, tokens, width = cotangent.shape
    rows = weight_t.shape[1]
    cols = min(2048, width)
    per = width // cols
    return pl.pallas_call(
        back_kernel,
        out_shape=jax.ShapeDtypeStruct((tokens, rows), jnp.bfloat16),
        grid=(tiles, per),
        in_specs=[
            pl.BlockSpec((1, tokens, cols), lambda f, j: (f, 0, j)),
            pl.BlockSpec((cols, rows), lambda f, j: (f * per + j, 0)),
        ],
        out_specs=pl.BlockSpec((tokens, rows), lambda f, j: (0, 0)),
        scratch_shapes=[pltpu.VMEM((tokens, rows), jnp.float32)],
        compiler_params=pltpu.CompilerParams(vmem_limit_bytes=VMEM),
        cost_estimate=pl.CostEstimate(
            flops=2 * tokens * rows * FF, bytes_accessed=2 * FF * (rows + tokens), transcendentals=0
        ),
    )(cotangent, weight_t)


def grad_kernel(scale, idx, x_ref, g_ref, o_ref, dense):
    groups, _, part, width = g_ref.shape
    block_rows, _, kept = o_ref.shape
    cols = min(512, width)
    per = width // cols
    base = pl.program_id(0) * block_rows

    @pl.loop(0, FF // cols)
    def _(c):
        at = pl.ds(pl.multiple_of((c % per) * cols, cols), cols)
        right = g_ref[:, c // per, :, at].reshape(groups * part, cols)
        dense[:, pl.ds(pl.multiple_of(c * cols, cols), cols)] = (
            jnp.dot(x_ref[...], right, preferred_element_type=jnp.float32) * scale
        )

    lane = lax.broadcasted_iota(jnp.int32, (BS, 2 * BS), 1)
    for i in range(block_rows):
        rows = slice(i * BS, (i + 1) * BS)

        @pl.loop(0, kept // (2 * BS), unroll=2)
        def _(q):
            low, high = idx[base + i, 2 * q], idx[base + i, 2 * q + 1]
            a = dense[rows, pl.ds(pl.multiple_of((low // 2) * (2 * BS), 2 * BS), 2 * BS)]
            b = dense[rows, pl.ds(pl.multiple_of((high // 2) * (2 * BS), 2 * BS), 2 * BS)]
            a = pltpu.roll(a, (low % 2) * BS, 1)
            b = pltpu.roll(b, ((high + 1) % 2) * BS, 1)
            o_ref[i, :, pl.ds(pl.multiple_of(q * 2 * BS, 2 * BS), 2 * BS)] = jnp.where(
                lane < BS, a, b
            )


def weight_gradient(col_idx, features_t, cotangent):
    rows, tokens = features_t.shape
    kept = col_idx.shape[1] * BS
    block_rows = min(4, rows // BS)
    return pl.pallas_call(
        functools.partial(grad_kernel, float(tokens) ** -0.5),
        out_shape=jax.ShapeDtypeStruct((rows // BS, BS, kept), jnp.float32),
        grid_spec=pltpu.PrefetchScalarGridSpec(
            num_scalar_prefetch=1,
            grid=(rows // BS // block_rows,),
            in_specs=[
                pl.BlockSpec((block_rows * BS, tokens), lambda i, idx: (i, 0)),
                pl.BlockSpec(
                    cotangent.shape, lambda i, idx: (0, 0, 0, 0), pipeline_mode=pl.Buffered(1)
                ),
            ],
            out_specs=pl.BlockSpec((block_rows, BS, kept), lambda i, idx: (i, 0, 0)),
            scratch_shapes=[pltpu.VMEM((block_rows * BS, FF), jnp.float32)],
        ),
        compiler_params=pltpu.CompilerParams(vmem_limit_bytes=VMEM),
        cost_estimate=pl.CostEstimate(
            flops=2 * tokens * rows * FF,
            bytes_accessed=2 * tokens * FF + 4 * rows * kept,
            transcendentals=0,
        ),
    )(col_idx, features_t, cotangent)


def body(features, values, col_idx, cotangent):
    tiles = lax.axis_size("fsdp")
    rows = values.shape[0] * BS
    token_cotangent = lax.all_gather(cotangent, "fsdp", axis=0)
    all_cotangent = lax.all_gather(token_cotangent, ("dp", "sub"), axis=0)
    all_features = lax.all_gather(features, ("dp", "sub"), axis=0, tiled=True)
    weight_t = expand(col_idx, values.reshape(rows, -1).T)
    partial = project(features, weight_t, tiles)
    projected = lax.psum_scatter(partial, "fsdp", scatter_dimension=0)
    input_grad = back(token_cotangent, weight_t)
    weight_grad = weight_gradient(col_idx, all_features.T, all_cotangent)
    return (projected, input_grad, weight_grad)


def solution(mesh):
    in_specs = (
        P(("rep", "dp", "sub"), "fsdp"),
        P("fsdp", None, None),
        P("fsdp", None),
        P(("rep", "dp", "sub"), "fsdp"),
    )
    out_specs = (
        P(("rep", "dp", "sub"), "fsdp"),
        P(("rep", "dp", "sub"), "fsdp"),
        P(("rep", "fsdp"), None, None),
    )
    return jax.shard_map(body, mesh=mesh, in_specs=in_specs, out_specs=out_specs, check_vma=False)
```

time: 2470 us -> 305 us (0.12)
  waiting for transfers between devices: 1470 us -> 139 us
  local copies, waits for them, and re-layouts: 746 us -> 15.8 us
  Pallas kernels: 0 us -> 136 us
  matrix products: 117 us -> 0 us
  other arithmetic: 91.6 us -> 0 us
    all_to_all x2 -> x0, waiting for transfers between devices: 1100 us -> none  [the longest x1 682 us: body(): lax.all_to_all(weight_grad_tile.reshape(D, 1, tile_width), 'fsdp', split_...]
    reshape x5 -> x1, local copies, waits for them, and re-layouts: 255 us -> 14 us  [body(): weight_t = expand(col_idx, values.reshape(rows, -1).T)]
    unnamed x16 -> x1, local copies, waits for them, and re-layouts: 186 us -> 1.79 us
    psum x1 -> x0, waiting for transfers between devices: 158 us -> none  [body(): grad_total = lax.psum(partial_grad, ('dp', 'sub')).astype(jnp.float32)]
    convert_element_type x2 -> x0, local copies, waits for them, and re-layouts: 137 us -> none  [the longest x1 113 us: body(): dense_rows = jnp.einsum('rkn,rakb->ranb', selector, values_view, preferre...]
    pallas_call x0 -> x4, Pallas kernels: none -> 136 us  [the longest x1 80.3 us: weight_gradient(): pl.pallas_call(functools.partial(grad_kernel, float(tokens) ** (-0.5)), o...]
    another operation x2 -> x0, local copies, waits for them, and re-layouts: 87.4 us -> none  [the longest x1 86.9 us: body(): dense_flat = dense_rows.reshape(rows_dev * BS, tile_count, tile_width)]
    all_to_all x2 -> x0, local copies, waits for them, and re-layouts: 80.6 us -> none  [the longest x1 40.6 us: body(): lax.all_to_all(weight_grad_tile.reshape(D, 1, tile_width), 'fsdp', split_...]
  transfers between devices with their start and end apart: 5 -> 4, of which waited for: 4 -> 2; matrix products, arithmetic and copies ran while one was open for 26% -> 5% of each run, Pallas kernels for 0% -> 45%
where the time goes in v1:
time: 305 us; the launch traced here: 304 us
  waiting for transfers between devices  139 us (46%)
  Pallas kernels  136 us (45%)
  local copies, waits for them, and re-layouts  15.8 us (5%)
  between operations  13.8 us (5%)
    all_gather x1, waiting for transfers between devices, body(): token_cotangent = lax.all_gather(cotangent, 'fsdp', axis=0)  83.3 us
    pallas_call x1, Pallas kernels, weight_gradient(): pl.pallas_call(functools.partial(grad_kernel, float(tokens) ** (-0.5)), o...  80.3 us
    all_gather x1, waiting for transfers between devices, body(): all_cotangent = lax.all_gather(token_cotangent, ('dp', 'sub'), axis=0)  54.5 us
    pallas_call x1, Pallas kernels, expand(): pl.pallas_call(expand_kernel, out_shape=jax.ShapeDtypeStruct((FF, rows),...  21.1 us
    pallas_call x1, Pallas kernels, project(): pl.pallas_call(project_kernel, out_shape=jax.ShapeDtypeStruct((tiles, tok...  19.2 us
    pallas_call x1, Pallas kernels, back(): pl.pallas_call(back_kernel, out_shape=jax.ShapeDtypeStruct((tokens, rows)...  15.5 us
    reshape x1, local copies, waits for them, and re-layouts, body(): weight_t = expand(col_idx, values.reshape(rows, -1).T)  14 us
  transfers between devices with their start and end apart: 4, of which 2 were waited for; matrix products, arithmetic and copies ran while one was open for 5% of the time, Pallas kernels for 45%

profile of v1, /device:TPU:0, one launch (start us, length us, event | category | flops | bytes accessed | tf_op | source)
XLA Modules:
  0.0 304.3 jit_solution(18270010920399726935)
XLA Ops:
  7.2 0.0 all-gather.8.cloned.1.call-start
  7.2 0.7 all-gather.8.cloned.1.call-update
  7.9 0.0 all-gather.6.cloned.1.call-start
  7.9 1.8 copy.12
  9.7 0.0 all-gather.6.cloned.1.call-update
  9.8 0.0 all-gather.10.cloned.1.call-start
  9.8 83.3 %all-gather.8.cloned.1.call-done = bf16[512,4096]{1,0:T(8,128)(2,1)} async-done(((bf16[128,4096]{1,0:T(8,128)(2,1)}), bf16[512,4096]{1,0:T(8,128)(2,1)}) %all-gather.8.cloned.1.call-update) | async-done | bytes 4194320 | tf_op jit(solution)/shard_map/all_gather | solution.py:183
  93.1 0.0 all-gather.10.cloned.1.call-update
  93.1 0.0 reduce-scatter.2.cloned.1.call-start
  93.1 14.0 %copy.11 = bf16[1024,4864]{0,1:T(8,128)(2,1)} copy(bf16[1024,4864]{1,0:T(8,128)(2,1)} %bitcast.9) | data formatting | bytes 19922944 | tf_op jit(solution)/shard_map/reshape | solution.py:186
  107.1 21.1 %shard_map.67.w_ref = bf16[16384,1024]{1,0:T(8,128)(2,1)} custom-call(s32[16,76]{1,0:T(8,128)} %idx.3, bf16[4864,1024]{1,0:T(8,128)(2,1)} %bitcast.6), custom_call_target="tpu_custom_call" | custom-call | bytes 43515904 | tf_op jit(solution)/shard_map/pallas_call | solution.py:40
  128.2 19.2 %shard_map.68 = bf16[4,128,4096]{2,1,0:T(8,128)(2,1)} custom-call(bf16[128,1024]{1,0:T(8,128)(2,1)} %x_ref.1, bf16[16384,1024]{1,0:T(8,128)(2,1)} %shard_map.67.w_ref), custom_call_target="tpu_custom_call" | custom-call | flops 4294967296 | bytes 37748736 | tf_op jit(solution)/shard_map/pallas_call | solution.py:67
  147.4 0.0 reduce-scatter.2.cloned.1.call-update
  147.5 15.5 %shard_map.69 = bf16[128,1024]{1,0:T(8,128)(2,1)} custom-call(bf16[4,128,4096]{2,1,0:T(8,128)(2,1)} %bitcast.8, bf16[16384,1024]{1,0:T(8,128)(2,1)} %shard_map.67.w_ref), custom_call_target="tpu_custom_call" | custom-call | flops 4294967296 | bytes 37748736 | tf_op jit(solution)/shard_map/pallas_call | solution.py:104
  163.0 0.0 all-gather.6.cloned.1.call-done
  163.0 54.5 %all-gather.10.cloned.1.call-done = bf16[16,128,4096]{2,1,0:T(8,128)(2,1)} async-done(((bf16[4,128,4096]{2,1,0:T(8,128)(2,1)}), bf16[16,128,4096]{2,1,0:T(8,128)(2,1)}) %all-gather.10.cloned.1.call-update) | async-done | bytes 16777232 | tf_op jit(solution)/shard_map/all_gather | solution.py:184
  217.5 80.3 %shard_map.70 = f32[16,64,4864]{2,1,0:T(8,128)} custom-call(s32[16,76]{1,0:T(8,128)} %idx.3, bf16[1024,512]{1,0:T(8,128)(2,1)} %bitcast.11, bf16[4,4,128,4096]{3,2,1,0:T(8,128)(2,1)} %bitcast.10), custom_call_target="tpu_custom_call" | custom-call | flops 17179869184 | bytes 36700160 | tf_op jit(solution)/shard_map/pallas_call | solution.py:156
  297.8 0.0 reduce-scatter.2.cloned.1.call-done
Async XLA Ops:
  7.2 85.9 %all-gather.8.cloned.1.call-start = ((), (), s32[]{:S(2)}) async-start(), calls=%async_computation.3 | async-start | bytes 5242880 | tf_op jit(solution)/shard_map/all_gather | solution.py:183
  7.9 155.1 %all-gather.6.cloned.1.call-start = ((), (), s32[]{:S(2)}) async-start(), calls=%async_computation.2 | async-start | bytes 1310720 | tf_op jit(solution)/shard_map/all_gather | solution.py:185
  9.8 207.8 %all-gather.10.cloned.1.call-start = ((), (), s32[]{:S(2)}) async-start(), calls=%async_computation.4 | async-start | bytes 20971520 | tf_op jit(solution)/shard_map/all_gather | solution.py:184
  93.1 204.7 %reduce-scatter.2.cloned.1.call-start = ((), (), s32[]{:S(2)}) async-start(), calls=%async_computation.1 | async-start | bytes 5242880 | tf_op jit(solution)/shard_map/reduce_scatter | solution.py:188
Sparse Core Ops, SparseCore 0:
  9.6 83.4 all-gather.7
  94.6 15.3 all-gather.5
  111.6 105.9 all-gather.9
  220.3 76.7 reduce-scatter.1

commit v2 on v1

v2 whole, which is shorter than its diff:
```python
import functools

import jax
import jax.numpy as jnp
from jax import lax
from jax.experimental import pallas as pl
from jax.experimental.pallas import tpu as pltpu
from jax.sharding import PartitionSpec as P

BS = 64
NBC = 256
FF = BS * NBC
VMEM = 60 * 1024 * 1024


def expand_kernel(idx, vt_ref, w_ref):
    pair = pl.program_id(0)
    keep = vt_ref.shape[0] // BS
    chunk = 512

    @pl.loop(0, FF // chunk)
    def _(i):
        w_ref[pl.ds(pl.multiple_of(i * chunk, chunk), chunk), :] = jnp.zeros(
            (chunk, 2 * BS), w_ref.dtype
        )

    lane = lax.broadcasted_iota(jnp.int32, (BS, 2 * BS), 1)
    for half in range(2):
        mask = (lane >= BS) if half else (lane < BS)

        @pl.loop(0, keep, unroll=4)
        def _(k):
            place = pl.ds(pl.multiple_of(idx[2 * pair + half, k] * BS, BS), BS)
            block = vt_ref[pl.ds(pl.multiple_of(k * BS, BS), BS), :]
            w_ref[place, :] = jnp.where(mask, block, w_ref[place, :])


def expand(col_idx, values_t):
    depth, rows = values_t.shape
    return pl.pallas_call(
        expand_kernel,
        out_shape=jax.ShapeDtypeStruct((FF, rows), values_t.dtype),
        grid_spec=pltpu.PrefetchScalarGridSpec(
            num_scalar_prefetch=1,
            grid=(rows // (2 * BS),),
            in_specs=[pl.BlockSpec((depth, 2 * BS), lambda i, idx: (0, i))],
            out_specs=pl.BlockSpec((FF, 2 * BS), lambda i, idx: (0, i)),
        ),
        compiler_params=pltpu.CompilerParams(vmem_limit_bytes=VMEM),
        cost_estimate=pl.CostEstimate(
            flops=0, bytes_accessed=2 * rows * (FF + depth), transcendentals=0
        ),
    )(col_idx, values_t)


def project_kernel(own, x_ref, w_ref, o_ref):
    o_ref[0] = lax.dot_general(
        x_ref[...], w_ref[...], (((1,), (1,)), ((), ())), preferred_element_type=jnp.float32
    ).astype(o_ref.dtype)


def project(own, features, weight_t, tiles):
    tokens, rows = features.shape
    width = FF // tiles
    cols = min(2048, width)
    per = width // cols
    return pl.pallas_call(
        project_kernel,
        out_shape=jax.ShapeDtypeStruct((tiles, tokens, width), jnp.bfloat16),
        grid_spec=pltpu.PrefetchScalarGridSpec(
            num_scalar_prefetch=1,
            grid=(tiles, per),
            in_specs=[
                pl.BlockSpec((tokens, rows), lambda d, j, own: (0, 0)),
                pl.BlockSpec(
                    (cols, rows), lambda d, j, own: (lax.rem(own[0] + d, tiles) * per + j, 0)
                ),
            ],
            out_specs=pl.BlockSpec((1, tokens, cols), lambda d, j, own: (d, 0, j)),
        ),
        compiler_params=pltpu.CompilerParams(vmem_limit_bytes=VMEM),
        cost_estimate=pl.CostEstimate(
            flops=2 * tokens * rows * FF, bytes_accessed=2 * FF * (rows + tokens), transcendentals=0
        ),
    )(own, features, weight_t)


def back_kernel(parts, *refs):
    w_ref, o_ref, total = refs[parts:]
    f = pl.program_id(0)

    @pl.when(f == 0)
    def _():
        total[...] = jnp.zeros_like(total)

    for h in range(parts):
        cols = refs[h].shape[2]
        total[...] += jnp.dot(
            refs[h][0], w_ref[h * cols : (h + 1) * cols, :], preferred_element_type=jnp.float32
        )

    @pl.when(f == pl.num_programs(0) - 1)
    def _():
        o_ref[...] = total[...].astype(o_ref.dtype)


def back(cotangents, weight_t):
    parts = len(cotangents)
    tiles, tokens, cols = cotangents[0].shape
    rows = weight_t.shape[1]
    return pl.pallas_call(
        functools.partial(back_kernel, parts),
        out_shape=jax.ShapeDtypeStruct((tokens, rows), jnp.bfloat16),
        grid=(tiles,),
        in_specs=[pl.BlockSpec((1, tokens, cols), lambda f: (f, 0, 0))] * parts
        + [pl.BlockSpec((parts * cols, rows), lambda f: (f, 0))],
        out_specs=pl.BlockSpec((tokens, rows), lambda f: (0, 0)),
        scratch_shapes=[pltpu.VMEM((tokens, rows), jnp.float32)],
        compiler_params=pltpu.CompilerParams(vmem_limit_bytes=VMEM),
        cost_estimate=pl.CostEstimate(
            flops=2 * tokens * rows * FF, bytes_accessed=2 * FF * (rows + tokens), transcendentals=0
        ),
    )(*cotangents, weight_t)


def grad_kernel(scale, parts, idx, x_ref, *refs):
    o_ref, dense = refs[-2:]
    pieces = refs[:-2]
    groups = len(pieces) // parts
    tiles, part, width = pieces[0].shape
    block_rows, _, kept = o_ref.shape
    cols = min(512, width)
    per = width // cols
    base = pl.program_id(0) * block_rows

    for h in range(parts):

        @pl.loop(0, tiles)
        def _(f):
            for j in range(per):
                at = pl.ds(j * cols, cols)
                right = jnp.concatenate(
                    [pieces[h * groups + t][f, :, at] for t in range(groups)], axis=0
                )
                place = pl.multiple_of((f * parts + h) * width + j * cols, cols)
                dense[:, pl.ds(place, cols)] = (
                    jnp.dot(x_ref[...], right, preferred_element_type=jnp.float32) * scale
                )

    lane = lax.broadcasted_iota(jnp.int32, (BS, 2 * BS), 1)

    @pl.loop(0, block_rows)
    def _(i):
        rows = pl.ds(pl.multiple_of(i * BS, BS), BS)
        for q in range(kept // (2 * BS)):
            low, high = idx[base + i, 2 * q], idx[base + i, 2 * q + 1]
            a = dense[rows, pl.ds(pl.multiple_of((low // 2) * (2 * BS), 2 * BS), 2 * BS)]
            b = dense[rows, pl.ds(pl.multiple_of((high // 2) * (2 * BS), 2 * BS), 2 * BS)]
            a = pltpu.roll(a, (low % 2) * BS, 1)
            b = pltpu.roll(b, ((high + 1) % 2) * BS, 1)
            o_ref[i, :, q * 2 * BS : (q + 1) * 2 * BS] = jnp.where(lane < BS, a, b)


def weight_gradient(col_idx, features_t, cotangents):
    rows, tokens = features_t.shape
    kept = col_idx.shape[1] * BS
    block_rows = min(4, rows // BS)
    flat = [piece for half in cotangents for piece in half]
    return pl.pallas_call(
        functools.partial(grad_kernel, float(tokens) ** -0.5, len(cotangents)),
        out_shape=jax.ShapeDtypeStruct((rows // BS, BS, kept), jnp.float32),
        grid_spec=pltpu.PrefetchScalarGridSpec(
            num_scalar_prefetch=1,
            grid=(rows // BS // block_rows,),
            in_specs=[pl.BlockSpec((block_rows * BS, tokens), lambda i, idx: (i, 0))]
            + [
                pl.BlockSpec(
                    flat[0].shape, lambda i, idx: (0, 0, 0), pipeline_mode=pl.Buffered(1)
                )
            ]
            * len(flat),
            out_specs=pl.BlockSpec((block_rows, BS, kept), lambda i, idx: (i, 0, 0)),
            scratch_shapes=[pltpu.VMEM((block_rows * BS, FF), jnp.float32)],
        ),
        compiler_params=pltpu.CompilerParams(vmem_limit_bytes=VMEM),
        cost_estimate=pl.CostEstimate(
            flops=2 * tokens * rows * FF,
            bytes_accessed=2 * tokens * FF + 4 * rows * kept,
            transcendentals=0,
        ),
    )(col_idx, features_t, *flat)


def shift(x, axis, by):
    size = lax.axis_size(axis)
    return lax.ppermute(x, axis, [(i, (i + by) % size) for i in range(size)])


def exchange(x):
    pieces = [x] + [shift(x, "dp", d) for d in range(1, lax.axis_size("dp"))]
    others = [shift(p, "sub", d) for d in range(1, lax.axis_size("sub")) for p in pieces]
    return pieces + others


def body(features, values, col_idx, cotangent):
    tiles = lax.axis_size("fsdp")
    rows = values.shape[0] * BS
    half = cotangent.shape[1] // 2
    halves = [
        lax.all_gather(cotangent[:, h * half : (h + 1) * half], "fsdp", axis=0) for h in range(2)
    ]
    all_features = jnp.concatenate(exchange(features), axis=0)
    weight_t = expand(col_idx, values.reshape(rows, -1).T)
    own = lax.axis_index("fsdp").astype(jnp.int32).reshape(1)
    partial = project(own, features, weight_t, tiles)
    total = partial[0].astype(jnp.float32)
    for d in range(1, tiles):
        total = total + shift(partial[d], "fsdp", d).astype(jnp.float32)
    projected = total.astype(jnp.bfloat16)
    input_grad = back(halves, weight_t)
    weight_grad = weight_gradient(col_idx, all_features.T, [exchange(h) for h in halves])
    return (projected, input_grad, weight_grad)


def solution(mesh):
    in_specs = (
        P(("rep", "dp", "sub"), "fsdp"),
        P("fsdp", None, None),
        P("fsdp", None),
        P(("rep", "dp", "sub"), "fsdp"),
    )
    out_specs = (
        P(("rep", "dp", "sub"), "fsdp"),
        P(("rep", "dp", "sub"), "fsdp"),
        P(("rep", "fsdp"), None, None),
    )
    return jax.shard_map(body, mesh=mesh, in_specs=in_specs, out_specs=out_specs, check_vma=False)
```

time: 305 us -> 289 us (0.948)
  Pallas kernels: 136 us -> 96.1 us
  starting transfers between devices: 0.16 us -> 9.86 us
  waiting for transfers between devices: 139 us -> 145 us
  other arithmetic: 0 us -> 3.96 us
    ppermute x0 -> x12, waiting for transfers between devices: none -> 88.1 us  [shift(): return lax.ppermute(x, axis, [(i, (i + by) % size) for i in range(size)])]
    all_gather x3 -> x2, waiting for transfers between devices: 138 us -> 55.7 us  [body(): lax.all_gather(cotangent[:, h * half:(h + 1) * half], 'fsdp', axis=0)]
    pallas_call x2, Pallas kernels: 95.8 us -> 57.4 us  [the longest x1 43.4 us: weight_gradient(): pl.pallas_call(functools.partial(grad_kernel, float(tokens) ** (-0.5), le...]
    ppermute x0 -> x12, starting transfers between devices: none -> 9.78 us  [shift(): return lax.ppermute(x, axis, [(i, (i + by) % size) for i in range(size)])]
  transfers between devices with their start and end apart: 4 -> 14, of which waited for: 2 -> 6; matrix products, arithmetic and copies ran while one was open for 5% -> 7% of each run, Pallas kernels for 45% -> 18%
where the time goes in v2:
time: 289 us; the launch traced here: 287 us
  waiting for transfers between devices  145 us (50%)
  Pallas kernels  96.1 us (33%)
  local copies, waits for them, and re-layouts  18.8 us (7%)
  between operations  14.1 us (5%)
  starting transfers between devices  9.86 us (3%)
  other arithmetic  3.96 us (1%)
    ppermute x12, waiting for transfers between devices, shift(): return lax.ppermute(x, axis, [(i, (i + by) % size) for i in range(size)])  88.1 us
    all_gather x2, waiting for transfers between devices, body(): lax.all_gather(cotangent[:, h * half:(h + 1) * half], 'fsdp', axis=0)  55.7 us
    pallas_call x1, Pallas kernels, weight_gradient(): pl.pallas_call(functools.partial(grad_kernel, float(tokens) ** (-0.5), le...  43.4 us
    pallas_call x1, Pallas kernels, expand(): pl.pallas_call(expand_kernel, out_shape=jax.ShapeDtypeStruct((FF, rows),...  20.5 us
    pallas_call x1, Pallas kernels, project(): pl.pallas_call(project_kernel, out_shape=jax.ShapeDtypeStruct((tiles, tok...  18.2 us
    pallas_call x1, Pallas kernels, back(): pl.pallas_call(functools.partial(back_kernel, parts), out_shape=jax.Shape...  14 us
    reshape x1, local copies, waits for them, and re-layouts, body(): weight_t = expand(col_idx, values.reshape(rows, -1).T)  14 us
    ppermute x12, starting transfers between devices, shift(): return lax.ppermute(x, axis, [(i, (i + by) % size) for i in range(size)])  9.78 us
  transfers between devices with their start and end apart: 14, of which 6 were waited for; matrix products, arithmetic and copies ran while one was open for 7% of the time, Pallas kernels for 18%

profile of v2, /device:TPU:0, one launch (start us, length us, event | category | flops | bytes accessed | tf_op | source)
XLA Modules:
  0.0 287.4 jit_solution(5234734412148978844)
XLA Ops:
  7.2 0.0 copy-start.1
  7.2 0.0 all-gather.5.cloned.1.call-start
  7.2 2.3 fusion.3
  9.5 0.0 all-gather.5.cloned.1.call-update
  9.5 0.0 all-gather.7.cloned.1.call-start
  9.6 0.7 all-gather.7.cloned.1.call-update
  10.3 0.0 copy-done.1
  10.3 0.2 copy.14
  10.5 3.0 %collective-permute-start.3 = (bf16[128,1024]{0,1:T(8,128)(2,1)S(1)}, bf16[128,1024]{0,1:T(8,128)(2,1)S(1)}, u32[]{:S(2)}, u32[]{:S(2)}) collective-permute-start(bf16[128,1024]{0,1:T(8,128)(2,1)S(1)} %copy.14), channel_id=1, source_target_pairs={{0,2},{2,0},{1,3},{3,1},{4,6},{6,4},{5,7},{7,5},{8,10},{10,8},{9,1... | collective-permute-start | bytes 786440 | tf_op jit(solution)/shard_map/ppermute | solution.py:196
  13.5 14.0 %copy.11 = bf16[1024,4864]{0,1:T(8,128)(2,1)} copy(bf16[1024,4864]{1,0:T(8,128)(2,1)} %bitcast.19) | data formatting | bytes 19922944 | tf_op jit(solution)/shard_map/reshape | solution.py:213
  27.5 20.5 %shard_map.67.w_ref.refs_2_ = bf16[16384,1024]{1,0:T(8,128)(2,1)} custom-call(s32[16,76]{1,0:T(8,128)} %idx.3, bf16[4864,1024]{1,0:T(8,128)(2,1)} %bitcast.18), custom_call_target="tpu_custom_call" | custom-call | bytes 43515904 | tf_op jit(solution)/shard_map/pallas_call | solution.py:40
  47.9 10.4 %all-gather.5.cloned.1.call-done = bf16[512,2048]{1,0:T(8,128)(2,1)} async-done(((bf16[128,2048]{1,0:T(8,128)(2,1)}), bf16[512,2048]{1,0:T(8,128)(2,1)}) %all-gather.5.cloned.1.call-update) | async-done | bytes 2097168 | tf_op jit(solution)/shard_map/all_gather | solution.py:210
  58.3 1.5 collective-permute-start.6
  59.8 45.4 %all-gather.7.cloned.1.call-done = bf16[512,2048]{1,0:T(8,128)(2,1)} async-done(((bf16[128,2048]{1,0:T(8,128)(2,1)}), bf16[512,2048]{1,0:T(8,128)(2,1)}) %all-gather.7.cloned.1.call-update) | async-done | bytes 2097168 | tf_op jit(solution)/shard_map/all_gather | solution.py:210
  105.2 1.5 collective-permute-start.9
  106.6 18.2 %shard_map.68 = bf16[4,128,4096]{2,1,0:T(8,128)(2,1)} custom-call(s32[1]{0:T(128)} %bitcast.own, bf16[128,1024]{1,0:T(8,128)(2,1)} %x_ref.1, bf16[16384,1024]{1,0:T(8,128)(2,1)} %shard_map.67.w_ref.refs_2_), custom_call_target="tpu_custom_call" | custom-call | flops 4294967296 | bytes 37748736 | tf_op jit(solution)/shard_map/pallas_call | solution.py:67
  124.9 0.0 copy-start
  124.9 2.3 slice_bitcast_fusion.2
  127.2 1.2 collective-permute-start.2
  128.4 0.2 collective-permute-start.1
  128.6 0.0 collective-permute-done.3
  128.6 0.0 collective-permute-start.4
  128.6 1.5 collective-permute-done.4
  130.1 0.1 collective-permute-start.5
  130.3 1.4 collective-permute-done.5
  131.7 1.7 collective-permute-start
  133.4 19.6 %collective-permute-done.2 = bf16[128,4096]{1,0:T(8,128)(2,1)S(1)} collective-permute-done((bf16[128,4096]{1,0:T(8,128)(2,1)S(1)}, bf16[128,4096]{1,0:T(8,128)(2,1)S(1)}, u32[]{:S(2)}, u32[]{:S(2)}) %collective-permute-start.2) | collective-permute-done | bytes 1048608 | tf_op jit(solution)/shard_map/ppermute | solution.py:196
  153.0 0.0 copy-done
  153.0 0.0 collective-permute-start.7
  153.0 65.6 %collective-permute-done.1 = bf16[128,4096]{1,0:T(8,128)(2,1)S(1)} collective-permute-done((bf16[128,4096]{1,0:T(8,128)(2,1)S(1)}, bf16[128,4096]{1,0:T(8,128)(2,1)S(1)}, u32[]{:S(2)}, u32[]{:S(2)}) %collective-permute-start.1) | collective-permute-done | bytes 1048608 | tf_op jit(solution)/shard_map/ppermute | solution.py:196
  218.6 0.0 collective-permute-start.10
  218.6 0.0 collective-permute-done.6.refs_1_
  218.6 0.5 collective-permute-start.8
  219.1 0.0 collective-permute-done.9.refs_5_
  219.1 0.1 collective-permute-start.11
  219.2 1.1 maximum_bitcast_fusion.x_ref
  220.3 0.0 collective-permute-done
  220.3 2.9 fusion.2
  223.2 14.0 %shard_map.69 = bf16[128,1024]{1,0:T(8,128)(2,1)} custom-call(bf16[4,128,2048]{2,1,0:T(8,128)(2,1)} %bitcast.21, bf16[4,128,2048]{2,1,0:T(8,128)(2,1)} %bitcast.8.refs_1_.refs_4_, bf16[16384,1024]{1,0:T(8,128)(2,1)} %shard_map.67.w_ref.refs_2_), custom_call_target="tpu_custom_call" | custom-call | flops 4294967296 | bytes 37748736 | tf_op jit(solution)/shard_map/pallas_call | solution.py:111
  237.1 0.0 collective-permute-done.7.refs_2_
  237.1 0.0 collective-permute-done.10.refs_6_
  237.2 0.0 collective-permute-done.8.refs_3_
  237.2 0.0 collective-permute-done.11.refs_7_
  237.2 43.4 %shard_map.70 = f32[16,64,4864]{2,1,0:T(8,128)} custom-call(s32[16,76]{1,0:T(8,128)} %idx.3, bf16[1024,512]{1,0:T(8,128)(2,1)} %maximum_bitcast_fusion.x_ref, bf16[4,128,2048]{2,1,0:T(8,128)(2,1)} %bitcast.22, bf16[4,128,2048]{2,1,0:T(8,128)(2,1)} %collective-permute-done.6.refs_1_, bf16[4,128,2048]{2,1,0:T(8,128)(2,1)} %collective-permute-done.7.refs_2_, ...), custom_call_target="tpu_custom_call" | custom-call | flops 17179869184 | bytes 36700160 | tf_op jit(solution)/shard_map/pallas_call | solution.py:169
Async XLA Ops:
  7.2 3.1 %copy-start.1 = (bf16[128,1024]{1,0:T(8,128)(2,1)S(1)}, bf16[128,1024]{1,0:T(8,128)(2,1)}, u32[]{:S(2)}) copy-start(bf16[128,1024]{1,0:T(8,128)(2,1)} %x_ref.1) | copy-start | bytes 786436
  7.2 51.2 %all-gather.5.cloned.1.call-start = ((), (), s32[]{:S(2)}) async-start(), calls=%async_computation | async-start | bytes 2621440 | tf_op jit(solution)/shard_map/all_gather | solution.py:210
  9.5 95.6 %all-gather.7.cloned.1.call-start = ((), (), s32[]{:S(2)}) async-start(), calls=%async_computation.1 | async-start | bytes 2621440 | tf_op jit(solution)/shard_map/all_gather | solution.py:210
  10.5 118.1 %collective-permute-start.3 = (bf16[128,1024]{0,1:T(8,128)(2,1)S(1)}, bf16[128,1024]{0,1:T(8,128)(2,1)S(1)}, u32[]{:S(2)}, u32[]{:S(2)}) collective-permute-start(bf16[128,1024]{0,1:T(8,128)(2,1)S(1)} %copy.14), channel_id=1, source_target_pairs={{0,2},{2,0},{1,3},{3,1},{4,6},{6,4},{5,7},{7,5},{8,10},{10,8},{9,1... | collective-permute-start | bytes 786440 | tf_op jit(solution)/shard_map/ppermute | solution.py:196
  58.3 160.3 %collective-permute-start.6 = (bf16[4,128,2048]{2,1,0:T(8,128)(2,1)}, bf16[4,128,2048]{2,1,0:T(8,128)(2,1)}, u32[]{:S(2)}, u32[]{:S(2)}) collective-permute-start(bf16[4,128,2048]{2,1,0:T(8,128)(2,1)} %bitcast.20), channel_id=1, source_target_pairs={{0,2},{2,0},{1,3},{3,1},{4,6},{6,4},{5,7},{7,5},{8,10},{10,8},{9,1... | collective-permute-start | bytes 6291464 | tf_op jit(solution)/shard_map/ppermute | solution.py:196
  105.2 114.0 %collective-permute-start.9 = (bf16[4,128,2048]{2,1,0:T(8,128)(2,1)}, bf16[4,128,2048]{2,1,0:T(8,128)(2,1)}, u32[]{:S(2)}, u32[]{:S(2)}) collective-permute-start(bf16[4,128,2048]{2,1,0:T(8,128)(2,1)} %bitcast.8.refs_1_.refs_4_), channel_id=1, source_target_pairs={{0,2},{2,0},{1,3},{3,1},{4,6},{6,4},{5,7},{7,5},{8,10},{10,8},{9,1... | collective-permute-start | bytes 6291464 | tf_op jit(solution)/shard_map/ppermute | solution.py:196
  124.9 28.1 %copy-start = (bf16[512,2048]{1,0:T(8,128)(2,1)S(1)}, bf16[512,2048]{1,0:T(8,128)(2,1)}, u32[]{:S(2)}) copy-start(bf16[512,2048]{1,0:T(8,128)(2,1)} %all-gather.5.cloned.1.call-done) | copy-start | bytes 6291460
  127.2 25.8 %collective-permute-start.2 = (bf16[128,4096]{1,0:T(8,128)(2,1)S(1)}, bf16[128,4096]{1,0:T(8,128)(2,1)S(1)}, u32[]{:S(2)}, u32[]{:S(2)}) collective-permute-start(bf16[128,4096]{1,0:T(8,128)(2,1)S(1)} %get-tuple-element.4), channel_id=1, source_target_pairs={{0,12},{4,0},{8,4},{12,8},{1,13},{5,1},{9,5},{13,9},{2,14},{6,2},{... | collective-permute-start | bytes 3145736 | tf_op jit(solution)/shard_map/ppermute | solution.py:196
  128.4 90.2 %collective-permute-start.1 = (bf16[128,4096]{1,0:T(8,128)(2,1)S(1)}, bf16[128,4096]{1,0:T(8,128)(2,1)S(1)}, u32[]{:S(2)}, u32[]{:S(2)}) collective-permute-start(bf16[128,4096]{1,0:T(8,128)(2,1)S(1)} %get-tuple-element.5), channel_id=1, source_target_pairs={{0,8},{4,12},{8,0},{12,4},{1,9},{5,13},{9,1},{13,5},{2,10},{6,14},... | collective-permute-start | bytes 3145736 | tf_op jit(solution)/shard_map/ppermute | solution.py:196
  128.6 1.5 collective-permute-start.4
  130.1 1.5 collective-permute-start.5
  131.7 88.6 %collective-permute-start = (bf16[128,4096]{1,0:T(8,128)(2,1)S(1)}, bf16[128,4096]{1,0:T(8,128)(2,1)S(1)}, u32[]{:S(2)}, u32[]{:S(2)}) collective-permute-start(bf16[128,4096]{1,0:T(8,128)(2,1)S(1)} %get-tuple-element.3), channel_id=1, source_target_pairs={{0,4},{4,8},{8,12},{12,0},{1,5},{5,9},{9,13},{13,1},{2,6},{6,10},{... | collective-permute-start | bytes 3145736 | tf_op jit(solution)/shard_map/ppermute | solution.py:196
  153.0 84.1 %collective-permute-start.7 = (bf16[4,128,2048]{2,1,0:T(8,128)(2,1)S(1)}, bf16[4,128,2048]{2,1,0:T(8,128)(2,1)}, u32[]{:S(2)}, u32[]{:S(2)}) collective-permute-start(bf16[4,128,2048]{2,1,0:T(8,128)(2,1)S(1)} %bitcast.23), channel_id=1, source_target_pairs={{0,1},{1,0},{2,3},{3,2},{4,5},{5,4},{6,7},{7,6},{8,9},{9,8},{10,11... | collective-permute-start | bytes 6291464 | tf_op jit(solution)/shard_map/ppermute | solution.py:196
  218.6 18.5 %collective-permute-start.10 = (bf16[4,128,2048]{2,1,0:T(8,128)(2,1)}, bf16[4,128,2048]{2,1,0:T(8,128)(2,1)}, u32[]{:S(2)}, u32[]{:S(2)}) collective-permute-start(bf16[4,128,2048]{2,1,0:T(8,128)(2,1)} %bitcast.8.refs_1_.refs_4_), channel_id=1, source_target_pairs={{0,1},{1,0},{2,3},{3,2},{4,5},{5,4},{6,7},{7,6},{8,9},{9,8},{10,11... | collective-permute-start | bytes 6291464 | tf_op jit(solution)/shard_map/ppermute | solution.py:196
  218.6 18.5 %collective-permute-start.8 = (bf16[4,128,2048]{2,1,0:T(8,128)(2,1)}, bf16[4,128,2048]{2,1,0:T(8,128)(2,1)}, u32[]{:S(2)}, u32[]{:S(2)}) collective-permute-start(bf16[4,128,2048]{2,1,0:T(8,128)(2,1)} %collective-permute-done.6.refs_1_), channel_id=1, source_target_pairs={{0,1},{1,0},{2,3},{3,2},{4,5},{5,4},{6,7},{7,6},{8,9},{9,8},{10,11... | collective-permute-start | bytes 6291464 | tf_op jit(solution)/shard_map/ppermute | solution.py:196
  219.1 18.0 %collective-permute-start.11 = (bf16[4,128,2048]{2,1,0:T(8,128)(2,1)}, bf16[4,128,2048]{2,1,0:T(8,128)(2,1)}, u32[]{:S(2)}, u32[]{:S(2)}) collective-permute-start(bf16[4,128,2048]{2,1,0:T(8,128)(2,1)} %collective-permute-done.9.refs_5_), channel_id=1, source_target_pairs={{0,1},{1,0},{2,3},{3,2},{4,5},{5,4},{6,7},{7,6},{8,9},{9,8},{10,11... | collective-permute-start | bytes 6291464 | tf_op jit(solution)/shard_map/ppermute | solution.py:196
Sparse Core Ops, SparseCore 0:
  9.7 48.6 all-gather.4
  60.5 44.6 all-gather.6

commit v3 on v2

--- a/solution.py
+++ b/solution.py
@@ -11,6 +11,7 @@
 NBC = 256
 FF = BS * NBC
 VMEM = 60 * 1024 * 1024
+PARTS = 4
 
 
 def expand_kernel(idx, vt_ref, w_ref):
@@ -53,13 +54,13 @@
     )(col_idx, values_t)
 
 
-def project_kernel(own, x_ref, w_ref, o_ref):
+def project_kernel(x_ref, w_ref, o_ref):
     o_ref[0] = lax.dot_general(
         x_ref[...], w_ref[...], (((1,), (1,)), ((), ())), preferred_element_type=jnp.float32
     ).astype(o_ref.dtype)
 
 
-def project(own, features, weight_t, tiles):
+def project(features, weight_t, tiles):
     tokens, rows = features.shape
     width = FF // tiles
     cols = min(2048, width)
@@ -67,22 +68,17 @@
     return pl.pallas_call(
         project_kernel,
         out_shape=jax.ShapeDtypeStruct((tiles, tokens, width), jnp.bfloat16),
-        grid_spec=pltpu.PrefetchScalarGridSpec(
-            num_scalar_prefetch=1,
-            grid=(tiles, per),
-            in_specs=[
-                pl.BlockSpec((tokens, rows), lambda d, j, own: (0, 0)),
-                pl.BlockSpec(
-                    (cols, rows), lambda d, j, own: (lax.rem(own[0] + d, tiles) * per + j, 0)
-                ),
-            ],
-            out_specs=pl.BlockSpec((1, tokens, cols), lambda d, j, own: (d, 0, j)),
-        ),
+        grid=(tiles, per),
+        in_specs=[
+            pl.BlockSpec((tokens, rows), lambda f, j: (0, 0)),
+            pl.BlockSpec((cols, rows), lambda f, j: (f * per + j, 0)),
+        ],
+        out_specs=pl.BlockSpec((1, tokens, cols), lambda f, j: (f, 0, j)),
         compiler_params=pltpu.CompilerParams(vmem_limit_bytes=VMEM),
         cost_estimate=pl.CostEstimate(
             flops=2 * tokens * rows * FF, bytes_accessed=2 * FF * (rows + tokens), transcendentals=0
         ),
-    )(own, features, weight_t)
+    )(features, weight_t)
 
 
 def back_kernel(parts, *refs):
@@ -205,20 +201,19 @@
 def body(features, values, col_idx, cotangent):
     tiles = lax.axis_size("fsdp")
     rows = values.shape[0] * BS
-    half = cotangent.shape[1] // 2
-    halves = [
-        lax.all_gather(cotangent[:, h * half : (h + 1) * half], "fsdp", axis=0) for h in range(2)
+    width = cotangent.shape[1] // PARTS
+    pieces = [
+        lax.all_gather(cotangent[:, h * width : (h + 1) * width], "fsdp", axis=0)
+        for h in range(PARTS)
     ]
     all_features = jnp.concatenate(exchange(features), axis=0)
     weight_t = expand(col_idx, values.reshape(rows, -1).T)
-    own = lax.axis_index("fsdp").astype(jnp.int32).reshape(1)
-    partial = project(own, features, weight_t, tiles)
-    total = partial[0].astype(jnp.float32)
-    for d in range(1, tiles):
-        total = total + shift(partial[d], "fsdp", d).astype(jnp.float32)
-    projected = total.astype(jnp.bfloat16)
-    input_grad = back(halves, weight_t)
-    weight_grad = weight_gradient(col_idx, all_features.T, [exchange(h) for h in halves])
+    partial = project(features, weight_t, tiles)
+    partial, pieces[1] = lax.optimization_barrier((partial, pieces[1]))
+    projected = lax.psum_scatter(partial, "fsdp", scatter_dimension=0)
+    input_grad = back(pieces, weight_t)
+    exchanged = [exchange(p) for p in pieces]
+    weight_grad = weight_gradient(col_idx, all_features.T, exchanged)
     return (projected, input_grad, weight_grad)
 
 

time: 289 us -> 244 us (0.84)
  waiting for transfers between devices: 145 us -> 101 us
  Pallas kernels: 96.1 us -> 102 us
    all_gather x2 -> x4, waiting for transfers between devices: 55.7 us -> 30.4 us  [body(): lax.all_gather(cotangent[:, h * width:(h + 1) * width], 'fsdp', axis=0)]
    ppermute x12 -> x15, waiting for transfers between devices: 88.1 us -> 68.3 us  [shift(): return lax.ppermute(x, axis, [(i, (i + by) % size) for i in range(size)])]
    pallas_call x1, Pallas kernels: 43.4 us -> 48.9 us  [weight_gradient(): pl.pallas_call(functools.partial(grad_kernel, float(tokens) ** (-0.5), le...]
    ppermute x12 -> x15, starting transfers between devices: 9.78 us -> 7.81 us  [shift(): return lax.ppermute(x, axis, [(i, (i + by) % size) for i in range(size)])]
  transfers between devices with their start and end apart: 14 -> 20, of which waited for: 6 -> 5; matrix products, arithmetic and copies ran while one was open for 7% -> 6% of each run, Pallas kernels for 18% -> 42%
where the time goes in v3:
time: 244 us; the launch traced here: 243 us
  Pallas kernels  102 us (42%)
  waiting for transfers between devices  101 us (41%)
  local copies, waits for them, and re-layouts  17.3 us (7%)
  between operations  13.9 us (6%)
  starting transfers between devices  8 us (3%)
    ppermute x15, waiting for transfers between devices, shift(): return lax.ppermute(x, axis, [(i, (i + by) % size) for i in range(size)])  68.3 us
    pallas_call x1, Pallas kernels, weight_gradient(): pl.pallas_call(functools.partial(grad_kernel, float(tokens) ** (-0.5), le...  48.9 us
    all_gather x4, waiting for transfers between devices, body(): lax.all_gather(cotangent[:, h * width:(h + 1) * width], 'fsdp', axis=0)  30.4 us
    pallas_call x1, Pallas kernels, expand(): pl.pallas_call(expand_kernel, out_shape=jax.ShapeDtypeStruct((FF, rows),...  20.5 us
    pallas_call x1, Pallas kernels, project(): pl.pallas_call(project_kernel, out_shape=jax.ShapeDtypeStruct((tiles, tok...  18.3 us
    pallas_call x1, Pallas kernels, back(): pl.pallas_call(functools.partial(back_kernel, parts), out_shape=jax.Shape...  14.2 us
    reshape x1, local copies, waits for them, and re-layouts, body(): weight_t = expand(col_idx, values.reshape(rows, -1).T)  14 us
    ppermute x15, starting transfers between devices, shift(): return lax.ppermute(x, axis, [(i, (i + by) % size) for i in range(size)])  7.81 us
  transfers between devices with their start and end apart: 20, of which 5 were waited for; matrix products, arithmetic and copies ran while one was open for 6% of the time, Pallas kernels for 42%

profile of v3, /device:TPU:0, one launch (start us, length us, event | category | flops | bytes accessed | tf_op | source)
XLA Modules:
  0.0 242.8 jit_solution(4701414912060467800)
XLA Ops:
  7.2 0.0 all-gather.9.cloned.1.call-start
  7.2 2.2 fusion
  9.4 0.0 all-gather.9.cloned.1.call-update
  9.4 0.0 all-gather.11.cloned.1.call-start
  9.5 0.7 all-gather.11.cloned.1.call-update
  10.2 0.0 all-gather.13.cloned.1.call-start
  10.2 0.7 all-gather.13.cloned.1.call-update
  10.9 0.0 all-gather.15.cloned.1.call-start
  10.9 0.5 all-gather.15.cloned.1.call-update
  11.5 0.0 reduce-scatter.2.cloned.1.call-start
  11.5 14.0 %copy.11 = bf16[1024,4864]{0,1:T(8,128)(2,1)} copy(bf16[1024,4864]{1,0:T(8,128)(2,1)} %bitcast.10) | data formatting | bytes 19922944 | tf_op jit(solution)/shard_map/reshape | solution.py:210
  25.5 20.5 %shard_map.67.w_ref.refs_4_ = bf16[16384,1024]{1,0:T(8,128)(2,1)} custom-call(s32[16,76]{1,0:T(8,128)} %idx.3, bf16[4864,1024]{1,0:T(8,128)(2,1)} %bitcast.9), custom_call_target="tpu_custom_call" | custom-call | bytes 43515904 | tf_op jit(solution)/shard_map/pallas_call | solution.py:41
  46.0 18.3 %shard_map.68 = bf16[4,128,4096]{2,1,0:T(8,128)(2,1)} custom-call(bf16[128,1024]{1,0:T(8,128)(2,1)} %x_ref.1, bf16[16384,1024]{1,0:T(8,128)(2,1)} %shard_map.67.w_ref.refs_4_), custom_call_target="tpu_custom_call" | custom-call | flops 4294967296 | bytes 37748736 | tf_op jit(solution)/shard_map/pallas_call | solution.py:68
  64.3 0.0 reduce-scatter.2.cloned.1.call-update
  64.3 5.5 %all-gather.11.cloned.1.call-done = bf16[512,1024]{1,0:T(8,128)(2,1)} async-done(((bf16[128,1024]{1,0:T(8,128)(2,1)}), bf16[512,1024]{1,0:T(8,128)(2,1)}) %all-gather.11.cloned.1.call-update) | async-done | bytes 1048592 | tf_op jit(solution)/shard_map/all_gather | solution.py:206
  69.8 1.5 collective-permute-start.3
  71.3 0.0 collective-permute-start.4
  71.3 0.2 copy.14
  71.5 0.6 collective-permute-start
  72.1 0.2 collective-permute-start.1
  72.3 28.1 %collective-permute-done = bf16[128,1024]{0,1:T(8,128)(2,1)S(1)} collective-permute-done((bf16[128,1024]{0,1:T(8,128)(2,1)S(1)}, bf16[128,1024]{0,1:T(8,128)(2,1)S(1)}, u32[]{:S(2)}, u32[]{:S(2)}) %collective-permute-start) | collective-permute-done | bytes 262176 | tf_op jit(solution)/shard_map/ppermute | solution.py:192
  100.4 0.0 collective-permute-start.2
  100.4 1.5 collective-permute-start.6
  101.9 0.0 collective-permute-done.1
  101.9 0.2 collective-permute-start.7
  102.1 0.0 collective-permute-done.2
  102.1 1.3 collective-permute-start.9
  103.4 0.0 collective-permute-done.3.refs_1_
  103.4 0.0 collective-permute-start.10
  103.4 24.9 %all-gather.15.cloned.1.call-done = bf16[512,1024]{1,0:T(8,128)(2,1)} async-done(((bf16[128,1024]{1,0:T(8,128)(2,1)}), bf16[512,1024]{1,0:T(8,128)(2,1)}) %all-gather.15.cloned.1.call-update) | async-done | bytes 1048592 | tf_op jit(solution)/shard_map/all_gather | solution.py:206
  128.3 0.0 collective-permute-done.4.refs_2_
  128.3 1.5 collective-permute-start.12
  129.8 0.0 collective-permute-done.6.refs_5_
  129.8 0.0 collective-permute-done.7.refs_6_
  129.8 0.5 collective-permute-start.5
  130.3 18.6 %collective-permute-done.9.refs_9_ = bf16[4,128,1024]{2,1,0:T(8,128)(2,1)} collective-permute-done((bf16[4,128,1024]{2,1,0:T(8,128)(2,1)}, bf16[4,128,1024]{2,1,0:T(8,128)(2,1)}, u32[]{:S(2)}, u32[]{:S(2)}) %collective-permute-start.9) | collective-permute-done | bytes 1048608 | tf_op jit(solution)/shard_map/ppermute | solution.py:192
  149.0 0.0 collective-permute-start.8
  149.0 0.0 collective-permute-done.10.refs_10_
  149.0 0.5 collective-permute-start.11
  149.5 21.6 %collective-permute-done.12.refs_13_ = bf16[4,128,1024]{2,1,0:T(8,128)(2,1)} collective-permute-done((bf16[4,128,1024]{2,1,0:T(8,128)(2,1)}, bf16[4,128,1024]{2,1,0:T(8,128)(2,1)}, u32[]{:S(2)}, u32[]{:S(2)}) %collective-permute-start.12) | collective-permute-done | bytes 1048608 | tf_op jit(solution)/shard_map/ppermute | solution.py:192
  171.0 0.0 collective-permute-start.14
  171.0 1.1 maximum_bitcast_fusion.x_ref
  172.2 14.2 %shard_map.69 = bf16[128,1024]{1,0:T(8,128)(2,1)} custom-call(bf16[4,128,1024]{2,1,0:T(8,128)(2,1)} %bitcast.17, bf16[4,128,1024]{2,1,0:T(8,128)(2,1)} %bitcast.11, bf16[4,128,1024]{2,1,0:T(8,128)(2,1)} %bitcast.21, bf16[4,128,1024]{2,1,0:T(8,128)(2,1)} %bitcast.25, bf16[16384,1024]{1,0:T(8,128)(2,1)} %shard_map.67.w_ref.refs_4_), custom_call_target="tpu_custom_call" | custom-call | flops 4294967296 | bytes 37748736 | tf_op jit(solution)/shard_map/pallas_call | solution.py:107
  186.3 0.0 collective-permute-done.5.refs_3_
  186.4 0.0 collective-permute-done.11.refs_11_
  186.4 0.0 collective-permute-done.14.refs_15_
  186.4 0.9 copy-done.3
  187.3 48.9 %shard_map.70 = f32[16,64,4864]{2,1,0:T(8,128)} custom-call(s32[16,76]{1,0:T(8,128)} %idx.3, bf16[1024,512]{1,0:T(8,128)(2,1)} %maximum_bitcast_fusion.x_ref, bf16[4,128,1024]{2,1,0:T(8,128)(2,1)} %bitcast.18, bf16[4,128,1024]{2,1,0:T(8,128)(2,1)} %copy-done.2, bf16[4,128,1024]{2,1,0:T(8,128)(2,1)} %collective-permute-done.4.refs_2_, ...), custom_call_target="tpu_custom_call" | custom-call | flops 17179869184 | bytes 36700160 | tf_op jit(solution)/shard_map/pallas_call | solution.py:165
  (13 shorter events, 0.0 us)
Async XLA Ops:
  7.2 57.1 %all-gather.9.cloned.1.call-start = ((), (), s32[]{:S(2)}) async-start(), calls=%async_computation.2 | async-start | bytes 1310720 | tf_op jit(solution)/shard_map/all_gather | solution.py:206
  9.4 60.4 %all-gather.11.cloned.1.call-start = ((), (), s32[]{:S(2)}) async-start(), calls=%async_computation.3 | async-start | bytes 1310720 | tf_op jit(solution)/shard_map/all_gather | solution.py:206
  10.2 92.0 %all-gather.13.cloned.1.call-start = ((), (), s32[]{:S(2)}) async-start(), calls=%async_computation.4 | async-start | bytes 1310720 | tf_op jit(solution)/shard_map/all_gather | solution.py:206
  10.9 117.4 %all-gather.15.cloned.1.call-start = ((), (), s32[]{:S(2)}) async-start(), calls=%async_computation.5 | async-start | bytes 1310720 | tf_op jit(solution)/shard_map/all_gather | solution.py:206
  11.5 224.8 %reduce-scatter.2.cloned.1.call-start = ((), (), s32[]{:S(2)}) async-start(), calls=%async_computation.1 | async-start | bytes 5242880 | tf_op jit(solution)/shard_map/reduce_scatter | solution.py:213
  64.3 7.0 %copy-start = (bf16[128,1024]{1,0:T(8,128)(2,1)S(1)}, bf16[128,1024]{1,0:T(8,128)(2,1)}, u32[]{:S(2)}) copy-start(bf16[128,1024]{1,0:T(8,128)(2,1)} %x_ref.1) | copy-start | bytes 786436
  64.3 36.1 %copy-start.1 = (bf16[512,1024]{1,0:T(8,128)(2,1)S(1)}, bf16[512,1024]{1,0:T(8,128)(2,1)}, u32[]{:S(2)}) copy-start(bf16[512,1024]{1,0:T(8,128)(2,1)} %all-gather.9.cloned.1.call-done) | copy-start | bytes 3145732
  69.8 33.6 %collective-permute-start.3 = (bf16[4,128,1024]{2,1,0:T(8,128)(2,1)}, bf16[4,128,1024]{2,1,0:T(8,128)(2,1)S(1)}, u32[]{:S(2)}, u32[]{:S(2)}) collective-permute-start(bf16[4,128,1024]{2,1,0:T(8,128)(2,1)} %bitcast.15), channel_id=1, source_target_pairs={{0,2},{2,0},{1,3},{3,1},{4,6},{6,4},{5,7},{7,5},{8,10},{10,8},{9,1... | collective-permute-start | bytes 3145736 | tf_op jit(solution)/shard_map/ppermute | solution.py:192
  71.3 57.0 %collective-permute-start.4 = (bf16[4,128,1024]{2,1,0:T(8,128)(2,1)}, bf16[4,128,1024]{2,1,0:T(8,128)(2,1)}, u32[]{:S(2)}, u32[]{:S(2)}) collective-permute-start(bf16[4,128,1024]{2,1,0:T(8,128)(2,1)} %bitcast.16), channel_id=1, source_target_pairs={{0,1},{1,0},{2,3},{3,2},{4,5},{5,4},{6,7},{7,6},{8,9},{9,8},{10,11... | collective-permute-start | bytes 3145736 | tf_op jit(solution)/shard_map/ppermute | solution.py:192
  71.5 28.9 %collective-permute-start = (bf16[128,1024]{0,1:T(8,128)(2,1)S(1)}, bf16[128,1024]{0,1:T(8,128)(2,1)S(1)}, u32[]{:S(2)}, u32[]{:S(2)}) collective-permute-start(bf16[128,1024]{0,1:T(8,128)(2,1)S(1)} %copy.14), channel_id=1, source_target_pairs={{0,2},{2,0},{1,3},{3,1},{4,6},{6,4},{5,7},{7,5},{8,10},{10,8},{9,1... | collective-permute-start | bytes 786440 | tf_op jit(solution)/shard_map/ppermute | solution.py:192
  72.1 29.8 %collective-permute-start.1 = (bf16[128,1024]{0,1:T(8,128)(2,1)S(1)}, bf16[128,1024]{0,1:T(8,128)(2,1)S(1)}, u32[]{:S(2)}, u32[]{:S(2)}) collective-permute-start(bf16[128,1024]{0,1:T(8,128)(2,1)S(1)} %copy.14), channel_id=1, source_target_pairs={{0,1},{1,0},{2,3},{3,2},{4,5},{5,4},{6,7},{7,6},{8,9},{9,8},{10,11... | collective-permute-start | bytes 786440 | tf_op jit(solution)/shard_map/ppermute | solution.py:192
  100.4 1.7 collective-permute-start.2
  100.4 29.4 %collective-permute-start.6 = (bf16[4,128,1024]{2,1,0:T(8,128)(2,1)S(1)}, bf16[4,128,1024]{2,1,0:T(8,128)(2,1)}, u32[]{:S(2)}, u32[]{:S(2)}) collective-permute-start(bf16[4,128,1024]{2,1,0:T(8,128)(2,1)S(1)} %bitcast.13), channel_id=1, source_target_pairs={{0,2},{2,0},{1,3},{3,1},{4,6},{6,4},{5,7},{7,5},{8,10},{10,8},{9,1... | collective-permute-start | bytes 3145736 | tf_op jit(solution)/shard_map/ppermute | solution.py:192
  101.9 27.9 %collective-permute-start.7 = (bf16[4,128,1024]{2,1,0:T(8,128)(2,1)S(1)}, bf16[4,128,1024]{2,1,0:T(8,128)(2,1)}, u32[]{:S(2)}, u32[]{:S(2)}) collective-permute-start(bf16[4,128,1024]{2,1,0:T(8,128)(2,1)S(1)} %bitcast.14), channel_id=1, source_target_pairs={{0,1},{1,0},{2,3},{3,2},{4,5},{5,4},{6,7},{7,6},{8,9},{9,8},{10,11... | collective-permute-start | bytes 3145736 | tf_op jit(solution)/shard_map/ppermute | solution.py:192
  102.1 46.8 %collective-permute-start.9 = (bf16[4,128,1024]{2,1,0:T(8,128)(2,1)}, bf16[4,128,1024]{2,1,0:T(8,128)(2,1)}, u32[]{:S(2)}, u32[]{:S(2)}) collective-permute-start(bf16[4,128,1024]{2,1,0:T(8,128)(2,1)} %bitcast.19), channel_id=1, source_target_pairs={{0,2},{2,0},{1,3},{3,1},{4,6},{6,4},{5,7},{7,5},{8,10},{10,8},{9,1... | collective-permute-start | bytes 3145736 | tf_op jit(solution)/shard_map/ppermute | solution.py:192
  103.4 82.9 %copy-start.2 = (bf16[4,128,1024]{2,1,0:T(8,128)(2,1)}, bf16[4,128,1024]{2,1,0:T(8,128)(2,1)S(1)}, u32[]{:S(2)}) copy-start(bf16[4,128,1024]{2,1,0:T(8,128)(2,1)S(1)} %collective-permute-done.3.refs_1_) | copy-start | bytes 3145732
  103.4 45.5 %collective-permute-start.10 = (bf16[4,128,1024]{2,1,0:T(8,128)(2,1)}, bf16[4,128,1024]{2,1,0:T(8,128)(2,1)}, u32[]{:S(2)}, u32[]{:S(2)}) collective-permute-start(bf16[4,128,1024]{2,1,0:T(8,128)(2,1)} %bitcast.20), channel_id=1, source_target_pairs={{0,1},{1,0},{2,3},{3,2},{4,5},{5,4},{6,7},{7,6},{8,9},{9,8},{10,11... | collective-permute-start | bytes 3145736 | tf_op jit(solution)/shard_map/ppermute | solution.py:192
  128.3 42.7 %collective-permute-start.12 = (bf16[4,128,1024]{2,1,0:T(8,128)(2,1)}, bf16[4,128,1024]{2,1,0:T(8,128)(2,1)}, u32[]{:S(2)}, u32[]{:S(2)}) collective-permute-start(bf16[4,128,1024]{2,1,0:T(8,128)(2,1)} %bitcast.23), channel_id=1, source_target_pairs={{0,2},{2,0},{1,3},{3,1},{4,6},{6,4},{5,7},{7,5},{8,10},{10,8},{9,1... | collective-permute-start | bytes 3145736 | tf_op jit(solution)/shard_map/ppermute | solution.py:192
  129.8 56.5 %collective-permute-start.13 = (bf16[4,128,1024]{2,1,0:T(8,128)(2,1)}, bf16[4,128,1024]{2,1,0:T(8,128)(2,1)}, u32[]{:S(2)}, u32[]{:S(2)}) collective-permute-start(bf16[4,128,1024]{2,1,0:T(8,128)(2,1)} %bitcast.24), channel_id=1, source_target_pairs={{0,1},{1,0},{2,3},{3,2},{4,5},{5,4},{6,7},{7,6},{8,9},{9,8},{10,11... | collective-permute-start | bytes 3145736 | tf_op jit(solution)/shard_map/ppermute | solution.py:192
  129.8 56.5 %collective-permute-start.5 = (bf16[4,128,1024]{2,1,0:T(8,128)(2,1)S(1)}, bf16[4,128,1024]{2,1,0:T(8,128)(2,1)S(1)}, u32[]{:S(2)}, u32[]{:S(2)}) collective-permute-start(bf16[4,128,1024]{2,1,0:T(8,128)(2,1)S(1)} %collective-permute-done.3.refs_1_), channel_id=1, source_target_pairs={{0,1},{1,0},{2,3},{3,2},{4,5},{5,4},{6,7},{7,6},{8,9},{9,8},{10,11... | collective-permute-start | bytes 3145736 | tf_op jit(solution)/shard_map/ppermute | solution.py:192
  149.0 37.4 %collective-permute-start.8 = (bf16[4,128,1024]{2,1,0:T(8,128)(2,1)}, bf16[4,128,1024]{2,1,0:T(8,128)(2,1)}, u32[]{:S(2)}, u32[]{:S(2)}) collective-permute-start(bf16[4,128,1024]{2,1,0:T(8,128)(2,1)} %collective-permute-done.6.refs_5_), channel_id=1, source_target_pairs={{0,1},{1,0},{2,3},{3,2},{4,5},{5,4},{6,7},{7,6},{8,9},{9,8},{10,11... | collective-permute-start | bytes 3145736 | tf_op jit(solution)/shard_map/ppermute | solution.py:192
  149.0 37.4 %collective-permute-start.11 = (bf16[4,128,1024]{2,1,0:T(8,128)(2,1)}, bf16[4,128,1024]{2,1,0:T(8,128)(2,1)}, u32[]{:S(2)}, u32[]{:S(2)}) collective-permute-start(bf16[4,128,1024]{2,1,0:T(8,128)(2,1)} %collective-permute-done.9.refs_9_), channel_id=1, source_target_pairs={{0,1},{1,0},{2,3},{3,2},{4,5},{5,4},{6,7},{7,6},{8,9},{9,8},{10,11... | collective-permute-start | bytes 3145736 | tf_op jit(solution)/shard_map/ppermute | solution.py:192
  171.0 15.3 %collective-permute-start.14 = (bf16[4,128,1024]{2,1,0:T(8,128)(2,1)}, bf16[4,128,1024]{2,1,0:T(8,128)(2,1)}, u32[]{:S(2)}, u32[]{:S(2)}) collective-permute-start(bf16[4,128,1024]{2,1,0:T(8,128)(2,1)} %collective-permute-done.12.refs_13_), channel_id=1, source_target_pairs={{0,1},{1,0},{2,3},{3,2},{4,5},{5,4},{6,7},{7,6},{8,9},{9,8},{10,11... | collective-permute-start | bytes 3145736 | tf_op jit(solution)/shard_map/ppermute | solution.py:192
  186.3 1.0 copy-start.3
Sparse Core Ops, SparseCore 0:
  10.1 30.6 all-gather.8
  42.4 27.4 all-gather.10
  71.4 27.4 all-gather.12
  100.9 27.4 all-gather.14
  131.0 76.2 reduce-scatter.1

commit v4 on v3

--- a/solution.py
+++ b/solution.py
@@ -11,7 +11,7 @@
 NBC = 256
 FF = BS * NBC
 VMEM = 60 * 1024 * 1024
-PARTS = 4
+PARTS = (2, 1, 1)
 
 
 def expand_kernel(idx, vt_ref, w_ref):
@@ -89,11 +89,13 @@
     def _():
         total[...] = jnp.zeros_like(total)
 
+    start = 0
     for h in range(parts):
         cols = refs[h].shape[2]
         total[...] += jnp.dot(
-            refs[h][0], w_ref[h * cols : (h + 1) * cols, :], preferred_element_type=jnp.float32
+            refs[h][0], w_ref[start : start + cols, :], preferred_element_type=jnp.float32
         )
+        start += cols
 
     @pl.when(f == pl.num_programs(0) - 1)
     def _():
@@ -102,14 +104,14 @@
 
 def back(cotangents, weight_t):
     parts = len(cotangents)
-    tiles, tokens, cols = cotangents[0].shape
+    tiles, tokens, _ = cotangents[0].shape
     rows = weight_t.shape[1]
     return pl.pallas_call(
         functools.partial(back_kernel, parts),
         out_shape=jax.ShapeDtypeStruct((tokens, rows), jnp.bfloat16),
         grid=(tiles,),
-        in_specs=[pl.BlockSpec((1, tokens, cols), lambda f: (f, 0, 0))] * parts
-        + [pl.BlockSpec((parts * cols, rows), lambda f: (f, 0))],
+        in_specs=[pl.BlockSpec((1, tokens, c.shape[2]), lambda f: (f, 0, 0)) for c in cotangents]
+        + [pl.BlockSpec((FF // tiles, rows), lambda f: (f, 0))],
         out_specs=pl.BlockSpec((tokens, rows), lambda f: (0, 0)),
         scratch_shapes=[pltpu.VMEM((tokens, rows), jnp.float32)],
         compiler_params=pltpu.CompilerParams(vmem_limit_bytes=VMEM),
@@ -123,25 +125,28 @@
     o_ref, dense = refs[-2:]
     pieces = refs[:-2]
     groups = len(pieces) // parts
-    tiles, part, width = pieces[0].shape
+    tiles = pieces[0].shape[0]
     block_rows, _, kept = o_ref.shape
-    cols = min(512, width)
-    per = width // cols
     base = pl.program_id(0) * block_rows
+    start = 0
 
     for h in range(parts):
+        width = pieces[h * groups].shape[2]
+        cols = min(512, width)
 
         @pl.loop(0, tiles)
-        def _(f):
-            for j in range(per):
+        def _(f, h=h, width=width, cols=cols, start=start):
+            for j in range(width // cols):
                 at = pl.ds(j * cols, cols)
                 right = jnp.concatenate(
                     [pieces[h * groups + t][f, :, at] for t in range(groups)], axis=0
                 )
-                place = pl.multiple_of((f * parts + h) * width + j * cols, cols)
+                place = pl.multiple_of(f * (FF // tiles) + start + j * cols, 128)
                 dense[:, pl.ds(place, cols)] = (
                     jnp.dot(x_ref[...], right, preferred_element_type=jnp.float32) * scale
                 )
+
+        start += width
 
     lane = lax.broadcasted_iota(jnp.int32, (BS, 2 * BS), 1)
 
@@ -170,11 +175,9 @@
             grid=(rows // BS // block_rows,),
             in_specs=[pl.BlockSpec((block_rows * BS, tokens), lambda i, idx: (i, 0))]
             + [
-                pl.BlockSpec(
-                    flat[0].shape, lambda i, idx: (0, 0, 0), pipeline_mode=pl.Buffered(1)
-                )
-            ]
-            * len(flat),
+                pl.BlockSpec(piece.shape, lambda i, idx: (0, 0, 0), pipeline_mode=pl.Buffered(1))
+                for piece in flat
+            ],
             out_specs=pl.BlockSpec((block_rows, BS, kept), lambda i, idx: (i, 0, 0)),
             scratch_shapes=[pltpu.VMEM((block_rows * BS, FF), jnp.float32)],
         ),
@@ -192,28 +195,40 @@
     return lax.ppermute(x, axis, [(i, (i + by) % size) for i in range(size)])
 
 
-def exchange(x):
-    pieces = [x] + [shift(x, "dp", d) for d in range(1, lax.axis_size("dp"))]
-    others = [shift(p, "sub", d) for d in range(1, lax.axis_size("sub")) for p in pieces]
-    return pieces + others
+def along_dp(x):
+    return [x] + [shift(x, "dp", d) for d in range(1, lax.axis_size("dp"))]
+
+
+def along_sub(pieces):
+    return pieces + [
+        shift(p, "sub", d) for d in range(1, lax.axis_size("sub")) for p in pieces
+    ]
 
 
 def body(features, values, col_idx, cotangent):
     tiles = lax.axis_size("fsdp")
     rows = values.shape[0] * BS
-    width = cotangent.shape[1] // PARTS
-    pieces = [
-        lax.all_gather(cotangent[:, h * width : (h + 1) * width], "fsdp", axis=0)
-        for h in range(PARTS)
-    ]
-    all_features = jnp.concatenate(exchange(features), axis=0)
-    weight_t = expand(col_idx, values.reshape(rows, -1).T)
+    unit = cotangent.shape[1] // sum(PARTS)
+    pieces, start = [], 0
+    for share in PARTS:
+        part = cotangent[:, start * unit : (start + share) * unit]
+        pieces.append(lax.all_gather(part, "fsdp", axis=0))
+        start += share
+    all_features = jnp.concatenate(along_sub(along_dp(features)), axis=0).T
+    values_t = values.reshape(rows, -1).T
+    values_t, all_features = lax.optimization_barrier((values_t, all_features))
+    weight_t = expand(col_idx, values_t)
     partial = project(features, weight_t, tiles)
-    partial, pieces[1] = lax.optimization_barrier((partial, pieces[1]))
+    partial, pieces[0] = lax.optimization_barrier((partial, pieces[0]))
     projected = lax.psum_scatter(partial, "fsdp", scatter_dimension=0)
+    columns = []
+    for h in range(len(PARTS)):
+        if h:
+            columns[-1], pieces[h] = lax.optimization_barrier((columns[-1], pieces[h]))
+        columns.append(along_dp(pieces[h]))
     input_grad = back(pieces, weight_t)
-    exchanged = [exchange(p) for p in pieces]
-    weight_grad = weight_gradient(col_idx, all_features.T, exchanged)
+    columns[-1], input_grad = lax.optimization_barrier((columns[-1], input_grad))
+    weight_grad = weight_gradient(col_idx, all_features, [along_sub(c) for c in columns])
     return (projected, input_grad, weight_grad)
 
 

time: 244 us -> 235 us (0.963)
  waiting for transfers between devices: 101 us -> 87.6 us
  local copies, waits for them, and re-layouts: 17.3 us -> 22.5 us
  Pallas kernels: 102 us -> 99.2 us
    all_gather x4 -> x3, waiting for transfers between devices: 30.4 us -> 8.37 us  [body(): pieces.append(lax.all_gather(part, 'fsdp', axis=0))]
    ppermute x15 -> x12, waiting for transfers between devices: 68.3 us -> 78.5 us  [shift(): return lax.ppermute(x, axis, [(i, (i + by) % size) for i in range(size)])]
    unnamed x9 -> x13, local copies, waits for them, and re-layouts: 1.12 us -> 4.73 us
    pallas_call x1, Pallas kernels: 48.9 us -> 46.2 us  [weight_gradient(): pl.pallas_call(functools.partial(grad_kernel, float(tokens) ** (-0.5), le...]
    ppermute x15 -> x12, starting transfers between devices: 7.81 us -> 9.14 us  [shift(): return lax.ppermute(x, axis, [(i, (i + by) % size) for i in range(size)])]
  transfers between devices with their start and end apart: 20 -> 16, of which waited for: 5 -> 6; matrix products, arithmetic and copies ran while one was open for 6% -> 7% of each run, Pallas kernels for 42% -> 42%
where the time goes in v4:
time: 235 us; the launch traced here: 233 us
  Pallas kernels  99.2 us (42%)
  waiting for transfers between devices  87.6 us (37%)
  local copies, waits for them, and re-layouts  22.5 us (10%)
  between operations  13.8 us (6%)
  starting transfers between devices  9.3 us (4%)
    ppermute x12, waiting for transfers between devices, shift(): return lax.ppermute(x, axis, [(i, (i + by) % size) for i in range(size)])  78.5 us
    pallas_call x1, Pallas kernels, weight_gradient(): pl.pallas_call(functools.partial(grad_kernel, float(tokens) ** (-0.5), le...  46.2 us
    pallas_call x1, Pallas kernels, expand(): pl.pallas_call(expand_kernel, out_shape=jax.ShapeDtypeStruct((FF, rows),...  20.5 us
    pallas_call x1, Pallas kernels, project(): pl.pallas_call(project_kernel, out_shape=jax.ShapeDtypeStruct((tiles, tok...  18.4 us
    pallas_call x1, Pallas kernels, back(): pl.pallas_call(functools.partial(back_kernel, parts), out_shape=jax.Shape...  14.1 us
    reshape x1, local copies, waits for them, and re-layouts, body(): values_t = values.reshape(rows, -1).T  14 us
    ppermute x12, starting transfers between devices, shift(): return lax.ppermute(x, axis, [(i, (i + by) % size) for i in range(size)])  9.14 us
    all_gather x3, waiting for transfers between devices, body(): pieces.append(lax.all_gather(part, 'fsdp', axis=0))  8.37 us
  transfers between devices with their start and end apart: 16, of which 6 were waited for; matrix products, arithmetic and copies ran while one was open for 7% of the time, Pallas kernels for 42%

profile of v4, /device:TPU:0, one launch (start us, length us, event | category | flops | bytes accessed | tf_op | source)
XLA Modules:
  0.0 233.5 jit_solution(5670578995265186794)
XLA Ops:
  7.2 0.0 copy-start.1
  7.2 0.0 all-gather.7.cloned.1.call-start
  7.2 1.9 slice.9
  9.1 0.0 all-gather.7.cloned.1.call-update
  9.2 0.0 all-gather.9.cloned.1.call-start
  9.2 1.8 fusion
  11.1 0.0 all-gather.9.cloned.1.call-update
  11.1 0.0 all-gather.11.cloned.1.call-start
  11.1 0.7 all-gather.11.cloned.1.call-update
  11.8 0.0 reduce-scatter.2.cloned.1.call-start
  11.9 0.0 copy-done.1
  11.9 0.2 copy.14
  12.1 3.0 %collective-permute-start = (bf16[128,1024]{0,1:T(8,128)(2,1)S(1)}, bf16[128,1024]{0,1:T(8,128)(2,1)S(1)}, u32[]{:S(2)}, u32[]{:S(2)}) collective-permute-start(bf16[128,1024]{0,1:T(8,128)(2,1)S(1)} %copy.14), channel_id=1, source_target_pairs={{0,2},{2,0},{1,3},{3,1},{4,6},{6,4},{5,7},{7,5},{8,10},{10,8},{9,1... | collective-permute-start | bytes 786440 | tf_op jit(solution)/shard_map/ppermute | solution.py:195
  15.1 0.0 collective-permute-start.1
  15.1 6.3 %collective-permute-done = bf16[128,1024]{0,1:T(8,128)(2,1)S(1)} collective-permute-done((bf16[128,1024]{0,1:T(8,128)(2,1)S(1)}, bf16[128,1024]{0,1:T(8,128)(2,1)S(1)}, u32[]{:S(2)}, u32[]{:S(2)}) %collective-permute-start) | collective-permute-done | bytes 262176 | tf_op jit(solution)/shard_map/ppermute | solution.py:195
  21.4 0.0 collective-permute-start.2
  21.4 14.0 %copy.11 = bf16[1024,4864]{0,1:T(8,128)(2,1)} copy(bf16[1024,4864]{1,0:T(8,128)(2,1)} %bitcast.9) | data formatting | bytes 19922944 | tf_op jit(solution)/shard_map/reshape | solution.py:218
  35.3 0.0 collective-permute-done.1
  35.3 0.0 collective-permute-done.2
  35.3 1.1 maximum_bitcast_fusion.x_ref
  36.4 20.5 %shard_map.67.w_ref.refs_3_ = bf16[16384,1024]{1,0:T(8,128)(2,1)} custom-call(s32[16,76]{1,0:T(8,128)} %idx.3, bf16[4864,1024]{1,0:T(8,128)(2,1)} %bitcast.8), custom_call_target="tpu_custom_call" | custom-call | bytes 43515904 | tf_op jit(solution)/shard_map/pallas_call | solution.py:41
  57.0 18.4 %shard_map.68 = bf16[4,128,4096]{2,1,0:T(8,128)(2,1)} custom-call(bf16[128,1024]{1,0:T(8,128)(2,1)} %x_ref.1, bf16[16384,1024]{1,0:T(8,128)(2,1)} %shard_map.67.w_ref.refs_3_), custom_call_target="tpu_custom_call" | custom-call | flops 4294967296 | bytes 37748736 | tf_op jit(solution)/shard_map/pallas_call | solution.py:68
  75.4 0.0 reduce-scatter.2.cloned.1.call-update
  75.4 1.6 copy-done
  77.0 1.7 collective-permute-start.3
  78.7 8.4 %all-gather.9.cloned.1.call-done = bf16[512,1024]{1,0:T(8,128)(2,1)} async-done(((bf16[128,1024]{1,0:T(8,128)(2,1)}), bf16[512,1024]{1,0:T(8,128)(2,1)}) %all-gather.9.cloned.1.call-update) | async-done | bytes 1048592 | tf_op jit(solution)/shard_map/all_gather | solution.py:215
  87.1 38.0 %collective-permute-done.3.refs_1_ = bf16[4,128,2048]{2,1,0:T(8,128)(2,1)} collective-permute-done((bf16[4,128,2048]{2,1,0:T(8,128)(2,1)S(1)}, bf16[4,128,2048]{2,1,0:T(8,128)(2,1)}, u32[]{:S(2)}, u32[]{:S(2)}) %collective-permute-start.3) | collective-permute-done | bytes 2097184 | tf_op jit(solution)/shard_map/ppermute | solution.py:195
  125.1 1.7 collective-permute-start.4
  126.8 0.0 collective-permute-start.6
  126.8 23.3 %collective-permute-done.4.refs_5_ = bf16[4,128,1024]{2,1,0:T(8,128)(2,1)S(1)} collective-permute-done((bf16[4,128,1024]{2,1,0:T(8,128)(2,1)}, bf16[4,128,1024]{2,1,0:T(8,128)(2,1)S(1)}, u32[]{:S(2)}, u32[]{:S(2)}) %collective-permute-start.4) | collective-permute-done | bytes 1048608 | tf_op jit(solution)/shard_map/ppermute | solution.py:195
  150.1 1.0 copy-done.3
  151.1 1.7 collective-permute-start.5
  152.8 0.0 collective-permute-start.7
  152.8 0.5 collective-permute-start.8
  153.3 0.0 collective-permute-start.9
  153.3 14.1 %shard_map.69 = bf16[128,1024]{1,0:T(8,128)(2,1)} custom-call(bf16[4,128,2048]{2,1,0:T(8,128)(2,1)} %bitcast.10, bf16[4,128,1024]{2,1,0:T(8,128)(2,1)} %bitcast.16, bf16[4,128,1024]{2,1,0:T(8,128)(2,1)} %bitcast.19, bf16[16384,1024]{1,0:T(8,128)(2,1)} %shard_map.67.w_ref.refs_3_), custom_call_target="tpu_custom_call" | custom-call | flops 4294967296 | bytes 37748736 | tf_op jit(solution)/shard_map/pallas_call | solution.py:109
  167.4 8.0 %collective-permute-done.5.refs_9_ = bf16[4,128,1024]{2,1,0:T(8,128)(2,1)} collective-permute-done((bf16[4,128,1024]{2,1,0:T(8,128)(2,1)}, bf16[4,128,1024]{2,1,0:T(8,128)(2,1)}, u32[]{:S(2)}, u32[]{:S(2)}) %collective-permute-start.5) | collective-permute-done | bytes 1048608 | tf_op jit(solution)/shard_map/ppermute | solution.py:195
  175.4 0.0 collective-permute-start.10
  175.4 0.0 collective-permute-done.6.refs_2_
  175.4 0.5 collective-permute-start.11
  175.9 0.0 collective-permute-done.7.refs_3_
  175.9 0.0 collective-permute-done.8.refs_6_
  175.9 0.0 collective-permute-done.9.refs_7_
  175.9 2.9 %collective-permute-done.10.refs_10_ = bf16[4,128,1024]{2,1,0:T(8,128)(2,1)S(1)} collective-permute-done((bf16[4,128,1024]{2,1,0:T(8,128)(2,1)S(1)}, bf16[4,128,1024]{2,1,0:T(8,128)(2,1)S(1)}, u32[]{:S(2)}, u32[]{:S(2)}) %collective-permute-start.10) | collective-permute-done | bytes 1048608 | tf_op jit(solution)/shard_map/ppermute | solution.py:195
  178.8 1.0 copy-done.4
  179.8 0.0 collective-permute-done.11.refs_11_
  179.8 1.0 copy-done.5
  180.8 46.2 %shard_map.70 = f32[16,64,4864]{2,1,0:T(8,128)} custom-call(s32[16,76]{1,0:T(8,128)} %idx.3, bf16[1024,512]{1,0:T(8,128)(2,1)} %maximum_bitcast_fusion.x_ref, bf16[4,128,2048]{2,1,0:T(8,128)(2,1)} %bitcast.11, bf16[4,128,2048]{2,1,0:T(8,128)(2,1)} %collective-permute-done.3.refs_1_, bf16[4,128,2048]{2,1,0:T(8,128)(2,1)} %collective-permute-done.6.refs_2_, ...), custom_call_target="tpu_custom_call" | custom-call | flops 17179869184 | bytes 36700160 | tf_op jit(solution)/shard_map/pallas_call | solution.py:170
  (9 shorter events, 0.0 us)
Async XLA Ops:
  7.2 4.7 %copy-start.1 = (bf16[128,1024]{1,0:T(8,128)(2,1)S(1)}, bf16[128,1024]{1,0:T(8,128)(2,1)}, u32[]{:S(2)}) copy-start(bf16[128,1024]{1,0:T(8,128)(2,1)} %x_ref.1) | copy-start | bytes 786436
  7.2 68.2 %all-gather.7.cloned.1.call-start = ((), (), s32[]{:S(2)}) async-start(), calls=%async_computation.2 | async-start | bytes 2621440 | tf_op jit(solution)/shard_map/all_gather | solution.py:215
  9.2 77.9 %all-gather.9.cloned.1.call-start = ((), (), s32[]{:S(2)}) async-start(), calls=%async_computation.3 | async-start | bytes 1310720 | tf_op jit(solution)/shard_map/all_gather | solution.py:215
  11.1 115.7 %all-gather.11.cloned.1.call-start = ((), (), s32[]{:S(2)}) async-start(), calls=%async_computation.4 | async-start | bytes 1310720 | tf_op jit(solution)/shard_map/all_gather | solution.py:215
  11.8 215.1 %reduce-scatter.2.cloned.1.call-start = ((), (), s32[]{:S(2)}) async-start(), calls=%async_computation.1 | async-start | bytes 5242880 | tf_op jit(solution)/shard_map/reduce_scatter | solution.py:223
  12.1 9.3 %collective-permute-start = (bf16[128,1024]{0,1:T(8,128)(2,1)S(1)}, bf16[128,1024]{0,1:T(8,128)(2,1)S(1)}, u32[]{:S(2)}, u32[]{:S(2)}) collective-permute-start(bf16[128,1024]{0,1:T(8,128)(2,1)S(1)} %copy.14), channel_id=1, source_target_pairs={{0,2},{2,0},{1,3},{3,1},{4,6},{6,4},{5,7},{7,5},{8,10},{10,8},{9,1... | collective-permute-start | bytes 786440 | tf_op jit(solution)/shard_map/ppermute | solution.py:195
  15.1 20.3 %collective-permute-start.1 = (bf16[128,1024]{0,1:T(8,128)(2,1)S(1)}, bf16[128,1024]{0,1:T(8,128)(2,1)S(1)}, u32[]{:S(2)}, u32[]{:S(2)}) collective-permute-start(bf16[128,1024]{0,1:T(8,128)(2,1)S(1)} %copy.14), channel_id=1, source_target_pairs={{0,1},{1,0},{2,3},{3,2},{4,5},{5,4},{6,7},{7,6},{8,9},{9,8},{10,11... | collective-permute-start | bytes 786440 | tf_op jit(solution)/shard_map/ppermute | solution.py:195
  21.4 14.0 %collective-permute-start.2 = (bf16[128,1024]{0,1:T(8,128)(2,1)S(1)}, bf16[128,1024]{0,1:T(8,128)(2,1)S(1)}, u32[]{:S(2)}, u32[]{:S(2)}) collective-permute-start(bf16[128,1024]{0,1:T(8,128)(2,1)S(1)} %collective-permute-done), channel_id=1, source_target_pairs={{0,1},{1,0},{2,3},{3,2},{4,5},{5,4},{6,7},{7,6},{8,9},{9,8},{10,11... | collective-permute-start | bytes 786440 | tf_op jit(solution)/shard_map/ppermute | solution.py:195
  75.4 1.6 copy-start
  77.0 48.1 %collective-permute-start.3 = (bf16[4,128,2048]{2,1,0:T(8,128)(2,1)S(1)}, bf16[4,128,2048]{2,1,0:T(8,128)(2,1)}, u32[]{:S(2)}, u32[]{:S(2)}) collective-permute-start(bf16[4,128,2048]{2,1,0:T(8,128)(2,1)S(1)} %bitcast.12), channel_id=1, source_target_pairs={{0,2},{2,0},{1,3},{3,1},{4,6},{6,4},{5,7},{7,5},{8,10},{10,8},{9,1... | collective-permute-start | bytes 6291464 | tf_op jit(solution)/shard_map/ppermute | solution.py:195
  125.1 25.0 %collective-permute-start.4 = (bf16[4,128,1024]{2,1,0:T(8,128)(2,1)}, bf16[4,128,1024]{2,1,0:T(8,128)(2,1)S(1)}, u32[]{:S(2)}, u32[]{:S(2)}) collective-permute-start(bf16[4,128,1024]{2,1,0:T(8,128)(2,1)} %bitcast.14), channel_id=1, source_target_pairs={{0,2},{2,0},{1,3},{3,1},{4,6},{6,4},{5,7},{7,5},{8,10},{10,8},{9,1... | collective-permute-start | bytes 3145736 | tf_op jit(solution)/shard_map/ppermute | solution.py:195
  126.8 48.6 %collective-permute-start.6 = (bf16[4,128,2048]{2,1,0:T(8,128)(2,1)S(1)}, bf16[4,128,2048]{2,1,0:T(8,128)(2,1)}, u32[]{:S(2)}, u32[]{:S(2)}) collective-permute-start(bf16[4,128,2048]{2,1,0:T(8,128)(2,1)S(1)} %bitcast.13), channel_id=1, source_target_pairs={{0,1},{1,0},{2,3},{3,2},{4,5},{5,4},{6,7},{7,6},{8,9},{9,8},{10,11... | collective-permute-start | bytes 6291464 | tf_op jit(solution)/shard_map/ppermute | solution.py:195
  150.1 1.0 copy-start.3
  151.1 24.3 %copy-start.2 = (bf16[512,1024]{1,0:T(8,128)(2,1)S(1)}, bf16[512,1024]{1,0:T(8,128)(2,1)}, u32[]{:S(2)}) copy-start(bf16[512,1024]{1,0:T(8,128)(2,1)} %all-gather.11.cloned.1.call-done) | copy-start | bytes 3145732
  151.1 24.3 %collective-permute-start.5 = (bf16[4,128,1024]{2,1,0:T(8,128)(2,1)}, bf16[4,128,1024]{2,1,0:T(8,128)(2,1)}, u32[]{:S(2)}, u32[]{:S(2)}) collective-permute-start(bf16[4,128,1024]{2,1,0:T(8,128)(2,1)} %bitcast.18), channel_id=1, source_target_pairs={{0,2},{2,0},{1,3},{3,1},{4,6},{6,4},{5,7},{7,5},{8,10},{10,8},{9,1... | collective-permute-start | bytes 3145736 | tf_op jit(solution)/shard_map/ppermute | solution.py:195
  152.8 23.2 %collective-permute-start.7 = (bf16[4,128,2048]{2,1,0:T(8,128)(2,1)}, bf16[4,128,2048]{2,1,0:T(8,128)(2,1)}, u32[]{:S(2)}, u32[]{:S(2)}) collective-permute-start(bf16[4,128,2048]{2,1,0:T(8,128)(2,1)} %collective-permute-done.3.refs_1_), channel_id=1, source_target_pairs={{0,1},{1,0},{2,3},{3,2},{4,5},{5,4},{6,7},{7,6},{8,9},{9,8},{10,11... | collective-permute-start | bytes 6291464 | tf_op jit(solution)/shard_map/ppermute | solution.py:195
  152.8 23.2 %collective-permute-start.8 = (bf16[4,128,1024]{2,1,0:T(8,128)(2,1)}, bf16[4,128,1024]{2,1,0:T(8,128)(2,1)}, u32[]{:S(2)}, u32[]{:S(2)}) collective-permute-start(bf16[4,128,1024]{2,1,0:T(8,128)(2,1)} %bitcast.15), channel_id=1, source_target_pairs={{0,1},{1,0},{2,3},{3,2},{4,5},{5,4},{6,7},{7,6},{8,9},{9,8},{10,11... | collective-permute-start | bytes 3145736 | tf_op jit(solution)/shard_map/ppermute | solution.py:195
  153.3 22.7 %collective-permute-start.9 = (bf16[4,128,1024]{2,1,0:T(8,128)(2,1)}, bf16[4,128,1024]{2,1,0:T(8,128)(2,1)}, u32[]{:S(2)}, u32[]{:S(2)}) collective-permute-start(bf16[4,128,1024]{2,1,0:T(8,128)(2,1)} %copy-done.3), channel_id=1, source_target_pairs={{0,1},{1,0},{2,3},{3,2},{4,5},{5,4},{6,7},{7,6},{8,9},{9,8},{10,11... | collective-permute-start | bytes 3145736 | tf_op jit(solution)/shard_map/ppermute | solution.py:195
  175.4 3.4 %collective-permute-start.10 = (bf16[4,128,1024]{2,1,0:T(8,128)(2,1)S(1)}, bf16[4,128,1024]{2,1,0:T(8,128)(2,1)S(1)}, u32[]{:S(2)}, u32[]{:S(2)}) collective-permute-start(bf16[4,128,1024]{2,1,0:T(8,128)(2,1)S(1)} %bitcast.21), channel_id=1, source_target_pairs={{0,1},{1,0},{2,3},{3,2},{4,5},{5,4},{6,7},{7,6},{8,9},{9,8},{10,11... | collective-permute-start | bytes 3145736 | tf_op jit(solution)/shard_map/ppermute | solution.py:195
  175.4 4.4 %collective-permute-start.11 = (bf16[4,128,1024]{2,1,0:T(8,128)(2,1)}, bf16[4,128,1024]{2,1,0:T(8,128)(2,1)S(1)}, u32[]{:S(2)}, u32[]{:S(2)}) collective-permute-start(bf16[4,128,1024]{2,1,0:T(8,128)(2,1)} %collective-permute-done.5.refs_9_), channel_id=1, source_target_pairs={{0,1},{1,0},{2,3},{3,2},{4,5},{5,4},{6,7},{7,6},{8,9},{9,8},{10,11... | collective-permute-start | bytes 3145736 | tf_op jit(solution)/shard_map/ppermute | solution.py:195
  178.8 1.0 copy-start.4
  179.8 1.0 copy-start.5
Sparse Core Ops, SparseCore 0:
  10.2 48.6 all-gather.6
  60.4 26.6 all-gather.8
  89.2 27.4 all-gather.10
  119.4 76.2 reduce-scatter.1

commit v5 on v4

--- a/solution.py
+++ b/solution.py
@@ -218,14 +218,17 @@
     values_t = values.reshape(rows, -1).T
     values_t, all_features = lax.optimization_barrier((values_t, all_features))
     weight_t = expand(col_idx, values_t)
+    weight_t, pieces[0] = lax.optimization_barrier((weight_t, pieces[0]))
+    columns = [along_dp(pieces[0])]
+    columns[0], pieces[1], weight_t = lax.optimization_barrier((columns[0], pieces[1], weight_t))
     partial = project(features, weight_t, tiles)
-    partial, pieces[0] = lax.optimization_barrier((partial, pieces[0]))
     projected = lax.psum_scatter(partial, "fsdp", scatter_dimension=0)
-    columns = []
-    for h in range(len(PARTS)):
-        if h:
-            columns[-1], pieces[h] = lax.optimization_barrier((columns[-1], pieces[h]))
+    for h in range(1, len(PARTS)):
         columns.append(along_dp(pieces[h]))
+        if h + 1 < len(PARTS):
+            columns[h], pieces[h + 1], partial = lax.optimization_barrier(
+                (columns[h], pieces[h + 1], partial)
+            )
     input_grad = back(pieces, weight_t)
     columns[-1], input_grad = lax.optimization_barrier((columns[-1], input_grad))
     weight_grad = weight_gradient(col_idx, all_features, [along_sub(c) for c in columns])

time: 235 us -> 234 us (level)
  local copies, waits for them, and re-layouts: 22.5 us -> 20.1 us
    all_gather x3, waiting for transfers between devices: 8.37 us -> 30.3 us  [body(): pieces.append(lax.all_gather(part, 'fsdp', axis=0))]
    ppermute x12, waiting for transfers between devices: 78.5 us -> 58.3 us  [shift(): return lax.ppermute(x, axis, [(i, (i + by) % size) for i in range(size)])]
    unnamed x13 -> x11, local copies, waits for them, and re-layouts: 4.73 us -> 3.27 us
  transfers between devices with their start and end apart: 16 -> 16, of which waited for: 6 -> 7; matrix products, arithmetic and copies ran while one was open for 7% -> 7% of each run, Pallas kernels for 42% -> 43%
where the time goes in v5:
time: 234 us; the launch traced here: 233 us
  Pallas kernels  99.7 us (43%)
  waiting for transfers between devices  88.6 us (38%)
  local copies, waits for them, and re-layouts  20.1 us (9%)
  between operations  13.8 us (6%)
  starting transfers between devices  9.18 us (4%)
    ppermute x12, waiting for transfers between devices, shift(): return lax.ppermute(x, axis, [(i, (i + by) % size) for i in range(size)])  58.3 us
    pallas_call x1, Pallas kernels, weight_gradient(): pl.pallas_call(functools.partial(grad_kernel, float(tokens) ** (-0.5), le...  46.2 us
    all_gather x3, waiting for transfers between devices, body(): pieces.append(lax.all_gather(part, 'fsdp', axis=0))  30.3 us
    pallas_call x1, Pallas kernels, expand(): pl.pallas_call(expand_kernel, out_shape=jax.ShapeDtypeStruct((FF, rows),...  20.5 us
    pallas_call x1, Pallas kernels, project(): pl.pallas_call(project_kernel, out_shape=jax.ShapeDtypeStruct((tiles, tok...  19 us
    pallas_call x1, Pallas kernels, back(): pl.pallas_call(functools.partial(back_kernel, parts), out_shape=jax.Shape...  14.1 us
    reshape x1, local copies, waits for them, and re-layouts, body(): values_t = values.reshape(rows, -1).T  14 us
    ppermute x12, starting transfers between devices, shift(): return lax.ppermute(x, axis, [(i, (i + by) % size) for i in range(size)])  9.02 us
  transfers between devices with their start and end apart: 16, of which 7 were waited for; matrix products, arithmetic and copies ran while one was open for 7% of the time, Pallas kernels for 43%

profile of v5, /device:TPU:0, one launch (start us, length us, event | category | flops | bytes accessed | tf_op | source)
XLA Modules:
  0.0 232.5 jit_solution(4884274085767093432)
XLA Ops:
  7.2 0.0 copy-start.2
  7.2 0.0 all-gather.7.cloned.1.call-start
  7.2 2.0 slice.9
  9.2 0.0 all-gather.7.cloned.1.call-update
  9.2 0.0 all-gather.9.cloned.1.call-start
  9.3 1.1 copy.14
  10.4 3.0 %collective-permute-start = (bf16[128,1024]{0,1:T(8,128)(2,1)S(1)}, bf16[128,1024]{0,1:T(8,128)(2,1)S(1)}, u32[]{:S(2)}, u32[]{:S(2)}) collective-permute-start(bf16[128,1024]{0,1:T(8,128)(2,1)S(1)} %copy.14), channel_id=1, source_target_pairs={{0,2},{2,0},{1,3},{3,1},{4,6},{6,4},{5,7},{7,5},{8,10},{10,8},{9,1... | collective-permute-start | bytes 786440 | tf_op jit(solution)/shard_map/ppermute | solution.py:195
  13.4 0.0 copy-done.2
  13.4 0.8 fusion
  14.2 0.0 all-gather.9.cloned.1.call-update
  14.2 0.0 all-gather.11.cloned.1.call-start
  14.3 0.1 collective-permute-start.1
  14.4 5.3 %collective-permute-done = bf16[128,1024]{0,1:T(8,128)(2,1)S(1)} collective-permute-done((bf16[128,1024]{0,1:T(8,128)(2,1)S(1)}, bf16[128,1024]{0,1:T(8,128)(2,1)S(1)}, u32[]{:S(2)}, u32[]{:S(2)}) %collective-permute-start) | collective-permute-done | bytes 262176 | tf_op jit(solution)/shard_map/ppermute | solution.py:195
  19.7 0.0 collective-permute-start.2
  19.7 14.0 %copy.11 = bf16[1024,4864]{0,1:T(8,128)(2,1)} copy(bf16[1024,4864]{1,0:T(8,128)(2,1)} %bitcast.9) | data formatting | bytes 19922944 | tf_op jit(solution)/shard_map/reshape | solution.py:218
  33.7 0.0 collective-permute-done.1
  33.7 0.0 collective-permute-done.2
  33.7 1.1 maximum_bitcast_fusion.x_ref
  34.8 20.5 %shard_map.67.w_ref.refs_3_ = bf16[16384,1024]{1,0:T(8,128)(2,1)} custom-call(s32[16,76]{1,0:T(8,128)} %idx.3, bf16[4864,1024]{1,0:T(8,128)(2,1)} %bitcast.8), custom_call_target="tpu_custom_call" | custom-call | bytes 43515904 | tf_op jit(solution)/shard_map/pallas_call | solution.py:41
  55.3 3.6 %all-gather.7.cloned.1.call-done = bf16[512,2048]{1,0:T(8,128)(2,1)} async-done(((bf16[128,2048]{1,0:T(8,128)(2,1)}), bf16[512,2048]{1,0:T(8,128)(2,1)}) %all-gather.7.cloned.1.call-update) | async-done | bytes 2097168 | tf_op jit(solution)/shard_map/all_gather | solution.py:215
  58.8 1.5 collective-permute-start.3
  60.3 0.0 all-gather.11.cloned.1.call-update
  60.3 0.0 reduce-scatter.2.cloned.1.call-start
  60.4 26.7 %all-gather.9.cloned.1.call-done = bf16[512,1024]{1,0:T(8,128)(2,1)} async-done(((bf16[128,1024]{1,0:T(8,128)(2,1)}), bf16[512,1024]{1,0:T(8,128)(2,1)}) %all-gather.9.cloned.1.call-update) | async-done | bytes 1048592 | tf_op jit(solution)/shard_map/all_gather | solution.py:215
  87.1 19.3 %collective-permute-done.3.refs_1_ = bf16[4,128,2048]{2,1,0:T(8,128)(2,1)S(1)} collective-permute-done((bf16[4,128,2048]{2,1,0:T(8,128)(2,1)}, bf16[4,128,2048]{2,1,0:T(8,128)(2,1)S(1)}, u32[]{:S(2)}, u32[]{:S(2)}) %collective-permute-start.3) | collective-permute-done | bytes 2097184 | tf_op jit(solution)/shard_map/ppermute | solution.py:195
  106.4 19.0 %shard_map.68 = bf16[4,128,4096]{2,1,0:T(8,128)(2,1)} custom-call(bf16[128,1024]{1,0:T(8,128)(2,1)} %x_ref.1, bf16[16384,1024]{1,0:T(8,128)(2,1)} %shard_map.67.w_ref.refs_3_), custom_call_target="tpu_custom_call" | custom-call | flops 4294967296 | bytes 37748736 | tf_op jit(solution)/shard_map/pallas_call | solution.py:68
  125.4 0.0 copy-done.3
  125.4 0.0 reduce-scatter.2.cloned.1.call-update
  125.5 1.2 copy-done.1
  126.7 1.5 collective-permute-start.4
  128.1 22.8 %collective-permute-done.4.refs_5_ = bf16[4,128,1024]{2,1,0:T(8,128)(2,1)} collective-permute-done((bf16[4,128,1024]{2,1,0:T(8,128)(2,1)S(1)}, bf16[4,128,1024]{2,1,0:T(8,128)(2,1)}, u32[]{:S(2)}, u32[]{:S(2)}) %collective-permute-start.4) | collective-permute-done | bytes 1048608 | tf_op jit(solution)/shard_map/ppermute | solution.py:195
  150.9 1.5 collective-permute-start.5
  152.4 0.0 collective-permute-start.6
  152.4 0.5 collective-permute-start.7
  152.9 0.0 collective-permute-start.8
  152.9 0.5 collective-permute-start.9
  153.4 14.1 %shard_map.69 = bf16[128,1024]{1,0:T(8,128)(2,1)} custom-call(bf16[4,128,2048]{2,1,0:T(8,128)(2,1)} %bitcast.11, bf16[4,128,1024]{2,1,0:T(8,128)(2,1)} %bitcast.14, bf16[4,128,1024]{2,1,0:T(8,128)(2,1)} %bitcast.19, bf16[16384,1024]{1,0:T(8,128)(2,1)} %shard_map.67.w_ref.refs_3_), custom_call_target="tpu_custom_call" | custom-call | flops 4294967296 | bytes 37748736 | tf_op jit(solution)/shard_map/pallas_call | solution.py:109
  167.5 7.0 %collective-permute-done.5.refs_9_ = bf16[4,128,1024]{2,1,0:T(8,128)(2,1)} collective-permute-done((bf16[4,128,1024]{2,1,0:T(8,128)(2,1)}, bf16[4,128,1024]{2,1,0:T(8,128)(2,1)}, u32[]{:S(2)}, u32[]{:S(2)}) %collective-permute-start.5) | collective-permute-done | bytes 1048608 | tf_op jit(solution)/shard_map/ppermute | solution.py:195
  174.4 0.0 collective-permute-start.10
  174.4 0.0 collective-permute-done.8.refs_6_
  174.4 0.5 collective-permute-start.11
  174.9 0.0 collective-permute-done.9.refs_7_
  174.9 0.0 collective-permute-done.6.refs_2_
  174.9 0.0 collective-permute-done.7.refs_3_
  174.9 3.9 %collective-permute-done.10.refs_10_ = bf16[4,128,1024]{2,1,0:T(8,128)(2,1)} collective-permute-done((bf16[4,128,1024]{2,1,0:T(8,128)(2,1)}, bf16[4,128,1024]{2,1,0:T(8,128)(2,1)}, u32[]{:S(2)}, u32[]{:S(2)}) %collective-permute-start.10) | collective-permute-done | bytes 1048608 | tf_op jit(solution)/shard_map/ppermute | solution.py:195
  178.9 0.0 collective-permute-done.11.refs_11_
  178.9 0.9 copy-done.4
  179.8 46.2 %shard_map.70 = f32[16,64,4864]{2,1,0:T(8,128)} custom-call(s32[16,76]{1,0:T(8,128)} %idx.3, bf16[1024,512]{1,0:T(8,128)(2,1)} %maximum_bitcast_fusion.x_ref, bf16[4,128,2048]{2,1,0:T(8,128)(2,1)} %bitcast.12, bf16[4,128,2048]{2,1,0:T(8,128)(2,1)} %copy-done.3, bf16[4,128,2048]{2,1,0:T(8,128)(2,1)} %collective-permute-done.6.refs_2_, ...), custom_call_target="tpu_custom_call" | custom-call | flops 17179869184 | bytes 36700160 | tf_op jit(solution)/shard_map/pallas_call | solution.py:170
  (7 shorter events, 0.0 us)
Async XLA Ops:
  7.2 6.2 %copy-start.2 = (bf16[128,4096]{1,0:T(8,128)(2,1)S(1)}, bf16[128,4096]{1,0:T(8,128)(2,1)}, u32[]{:S(2)}) copy-start(bf16[128,4096]{1,0:T(8,128)(2,1)} %param.7) | copy-start | bytes 3145732
  7.2 51.6 %all-gather.7.cloned.1.call-start = ((), (), s32[]{:S(2)}) async-start(), calls=%async_computation.2 | async-start | bytes 2621440 | tf_op jit(solution)/shard_map/all_gather | solution.py:215
  9.2 77.9 %all-gather.9.cloned.1.call-start = ((), (), s32[]{:S(2)}) async-start(), calls=%async_computation.3 | async-start | bytes 1310720 | tf_op jit(solution)/shard_map/all_gather | solution.py:215
  10.4 9.3 %collective-permute-start = (bf16[128,1024]{0,1:T(8,128)(2,1)S(1)}, bf16[128,1024]{0,1:T(8,128)(2,1)S(1)}, u32[]{:S(2)}, u32[]{:S(2)}) collective-permute-start(bf16[128,1024]{0,1:T(8,128)(2,1)S(1)} %copy.14), channel_id=1, source_target_pairs={{0,2},{2,0},{1,3},{3,1},{4,6},{6,4},{5,7},{7,5},{8,10},{10,8},{9,1... | collective-permute-start | bytes 786440 | tf_op jit(solution)/shard_map/ppermute | solution.py:195
  14.2 113.9 %all-gather.11.cloned.1.call-start = ((), (), s32[]{:S(2)}) async-start(), calls=%async_computation.4 | async-start | bytes 1310720 | tf_op jit(solution)/shard_map/all_gather | solution.py:215
  14.3 19.4 %collective-permute-start.1 = (bf16[128,1024]{0,1:T(8,128)(2,1)S(1)}, bf16[128,1024]{0,1:T(8,128)(2,1)S(1)}, u32[]{:S(2)}, u32[]{:S(2)}) collective-permute-start(bf16[128,1024]{0,1:T(8,128)(2,1)S(1)} %copy.14), channel_id=1, source_target_pairs={{0,1},{1,0},{2,3},{3,2},{4,5},{5,4},{6,7},{7,6},{8,9},{9,8},{10,11... | collective-permute-start | bytes 786440 | tf_op jit(solution)/shard_map/ppermute | solution.py:195
  19.7 14.0 %collective-permute-start.2 = (bf16[128,1024]{0,1:T(8,128)(2,1)S(1)}, bf16[128,1024]{0,1:T(8,128)(2,1)S(1)}, u32[]{:S(2)}, u32[]{:S(2)}) collective-permute-start(bf16[128,1024]{0,1:T(8,128)(2,1)S(1)} %collective-permute-done), channel_id=1, source_target_pairs={{0,1},{1,0},{2,3},{3,2},{4,5},{5,4},{6,7},{7,6},{8,9},{9,8},{10,11... | collective-permute-start | bytes 786440 | tf_op jit(solution)/shard_map/ppermute | solution.py:195
  58.8 47.6 %collective-permute-start.3 = (bf16[4,128,2048]{2,1,0:T(8,128)(2,1)}, bf16[4,128,2048]{2,1,0:T(8,128)(2,1)S(1)}, u32[]{:S(2)}, u32[]{:S(2)}) collective-permute-start(bf16[4,128,2048]{2,1,0:T(8,128)(2,1)} %bitcast.10), channel_id=1, source_target_pairs={{0,2},{2,0},{1,3},{3,1},{4,6},{6,4},{5,7},{7,5},{8,10},{10,8},{9,1... | collective-permute-start | bytes 6291464 | tf_op jit(solution)/shard_map/ppermute | solution.py:195
  60.3 165.7 %reduce-scatter.2.cloned.1.call-start = ((), (), s32[]{:S(2)}) async-start(), calls=%async_computation.1 | async-start | bytes 5242880 | tf_op jit(solution)/shard_map/reduce_scatter | solution.py:225
  106.4 19.0 %copy-start.3 = (bf16[4,128,2048]{2,1,0:T(8,128)(2,1)}, bf16[4,128,2048]{2,1,0:T(8,128)(2,1)S(1)}, u32[]{:S(2)}) copy-start(bf16[4,128,2048]{2,1,0:T(8,128)(2,1)S(1)} %collective-permute-done.3.refs_1_) | copy-start | bytes 6291460
  125.4 1.2 copy-start.1
  125.4 26.9 %copy-start = (bf16[512,2048]{1,0:T(8,128)(2,1)S(1)}, bf16[512,2048]{1,0:T(8,128)(2,1)}, u32[]{:S(2)}) copy-start(bf16[512,2048]{1,0:T(8,128)(2,1)} %all-gather.7.cloned.1.call-done) | copy-start | bytes 6291460
  126.7 24.2 %collective-permute-start.4 = (bf16[4,128,1024]{2,1,0:T(8,128)(2,1)S(1)}, bf16[4,128,1024]{2,1,0:T(8,128)(2,1)}, u32[]{:S(2)}, u32[]{:S(2)}) collective-permute-start(bf16[4,128,1024]{2,1,0:T(8,128)(2,1)S(1)} %bitcast.16), channel_id=1, source_target_pairs={{0,2},{2,0},{1,3},{3,1},{4,6},{6,4},{5,7},{7,5},{8,10},{10,8},{9,1... | collective-permute-start | bytes 3145736 | tf_op jit(solution)/shard_map/ppermute | solution.py:195
  150.9 23.5 %collective-permute-start.5 = (bf16[4,128,1024]{2,1,0:T(8,128)(2,1)}, bf16[4,128,1024]{2,1,0:T(8,128)(2,1)}, u32[]{:S(2)}, u32[]{:S(2)}) collective-permute-start(bf16[4,128,1024]{2,1,0:T(8,128)(2,1)} %bitcast.18), channel_id=1, source_target_pairs={{0,2},{2,0},{1,3},{3,1},{4,6},{6,4},{5,7},{7,5},{8,10},{10,8},{9,1... | collective-permute-start | bytes 3145736 | tf_op jit(solution)/shard_map/ppermute | solution.py:195
  152.4 22.6 %collective-permute-start.6 = (bf16[4,128,2048]{2,1,0:T(8,128)(2,1)S(1)}, bf16[4,128,2048]{2,1,0:T(8,128)(2,1)}, u32[]{:S(2)}, u32[]{:S(2)}) collective-permute-start(bf16[4,128,2048]{2,1,0:T(8,128)(2,1)S(1)} %bitcast.13), channel_id=1, source_target_pairs={{0,1},{1,0},{2,3},{3,2},{4,5},{5,4},{6,7},{7,6},{8,9},{9,8},{10,11... | collective-permute-start | bytes 6291464 | tf_op jit(solution)/shard_map/ppermute | solution.py:195
  152.4 22.6 %collective-permute-start.7 = (bf16[4,128,2048]{2,1,0:T(8,128)(2,1)}, bf16[4,128,2048]{2,1,0:T(8,128)(2,1)}, u32[]{:S(2)}, u32[]{:S(2)}) collective-permute-start(bf16[4,128,2048]{2,1,0:T(8,128)(2,1)} %copy-done.3), channel_id=1, source_target_pairs={{0,1},{1,0},{2,3},{3,2},{4,5},{5,4},{6,7},{7,6},{8,9},{9,8},{10,11... | collective-permute-start | bytes 6291464 | tf_op jit(solution)/shard_map/ppermute | solution.py:195
  152.9 21.5 %collective-permute-start.8 = (bf16[4,128,1024]{2,1,0:T(8,128)(2,1)S(1)}, bf16[4,128,1024]{2,1,0:T(8,128)(2,1)}, u32[]{:S(2)}, u32[]{:S(2)}) collective-permute-start(bf16[4,128,1024]{2,1,0:T(8,128)(2,1)S(1)} %bitcast.17), channel_id=1, source_target_pairs={{0,1},{1,0},{2,3},{3,2},{4,5},{5,4},{6,7},{7,6},{8,9},{9,8},{10,11... | collective-permute-start | bytes 3145736 | tf_op jit(solution)/shard_map/ppermute | solution.py:195
  152.9 22.1 %collective-permute-start.9 = (bf16[4,128,1024]{2,1,0:T(8,128)(2,1)}, bf16[4,128,1024]{2,1,0:T(8,128)(2,1)}, u32[]{:S(2)}, u32[]{:S(2)}) collective-permute-start(bf16[4,128,1024]{2,1,0:T(8,128)(2,1)} %collective-permute-done.4.refs_5_), channel_id=1, source_target_pairs={{0,1},{1,0},{2,3},{3,2},{4,5},{5,4},{6,7},{7,6},{8,9},{9,8},{10,11... | collective-permute-start | bytes 3145736 | tf_op jit(solution)/shard_map/ppermute | solution.py:195
  174.4 4.4 %collective-permute-start.10 = (bf16[4,128,1024]{2,1,0:T(8,128)(2,1)}, bf16[4,128,1024]{2,1,0:T(8,128)(2,1)}, u32[]{:S(2)}, u32[]{:S(2)}) collective-permute-start(bf16[4,128,1024]{2,1,0:T(8,128)(2,1)} %bitcast.20), channel_id=1, source_target_pairs={{0,1},{1,0},{2,3},{3,2},{4,5},{5,4},{6,7},{7,6},{8,9},{9,8},{10,11... | collective-permute-start | bytes 3145736 | tf_op jit(solution)/shard_map/ppermute | solution.py:195
  174.4 4.4 %collective-permute-start.11 = (bf16[4,128,1024]{2,1,0:T(8,128)(2,1)}, bf16[4,128,1024]{2,1,0:T(8,128)(2,1)S(1)}, u32[]{:S(2)}, u32[]{:S(2)}) collective-permute-start(bf16[4,128,1024]{2,1,0:T(8,128)(2,1)} %collective-permute-done.5.refs_9_), channel_id=1, source_target_pairs={{0,1},{1,0},{2,3},{3,2},{4,5},{5,4},{6,7},{7,6},{8,9},{9,8},{10,11... | collective-permute-start | bytes 3145736 | tf_op jit(solution)/shard_map/ppermute | solution.py:195
  178.9 0.9 copy-start.4
Sparse Core Ops, SparseCore 0:
  10.1 48.6 all-gather.6
  60.4 26.6 all-gather.8
  89.2 27.4 all-gather.10
  125.6 75.6 reduce-scatter.1
